TPU v7x, 256 devices: a whole 4x4x8 slice. The times are simulated.
256 devices in a mesh: gz: 16 (over y, z_hi), gx: 8 (over x, core), gy: 2 (over z_lo).
Axes of the slice: x: 4, y: 4, z: 8 (z_hi: 4, z_lo: 2; z = z_hi * 2 + z_lo), core: 2. Of those that a mesh axis runs over, the one named last changes fastest.
Arguments:
- electric: float32 [3, 256, 128, 256], P(None, 'gz', 'gx', 'gy'), may hold values from -6 to 6
- magnetic: float32 [3, 256, 128, 256], P(None, 'gz', 'gx', 'gy'), may hold values from -6 to 6
- aux_state: float32 [4, 2, 8, 128, 256], P(None, None, None, 'gx', 'gy'), may hold values from -6 to 6
- material: int32 [128, 256], P('gx', 'gy'), may hold values 0 or 1
- kerr_strength: float32 [2], replicated, may hold values from 0.1 to 1
Outputs:
- electric_out: float32 [3, 256, 128, 256], P(None, 'gz', 'gx', 'gy')
- magnetic_out: float32 [3, 256, 128, 256], P(None, 'gz', 'gx', 'gy')
Inputs may be any that keep to these rules, and one draw needn't show every extreme that they name: `material`: 0 marks cladding, 1 the waveguide core.
All inputs are finite; a program needn't handle non-finite values. No bound on the sum of `material` on one device may be relied on, other than what follows from the above.
Results may differ from a plain program's by a relative error of at most 0.00002.
Values sent between devices are 32-bit elements; how exact they have to be, the bound alone decides.
No kernel may reach another device: no remote copies, remote signals or barrier semaphores. Data moves between devices by JAX's collectives and lax.ppermute only.
A program may use at most 128 MiB of HBM per device.

v0:
```python
import jax
import jax.numpy as jnp
from jax import lax
from jax.sharding import PartitionSpec as P

PML = 8
STEPS = 4


courant = 0.5
pml_rate = 3.0
eps_clad = 2.085
eps_core = 4.0


def from_behind(shard, axis, by):
    length = lax.axis_size(axis)
    pairs = [(i, i + by) for i in range(length) if 0 <= i + by < length]
    return lax.ppermute(shard, axis, pairs)


def shifted(value, axis, steps):
    count = lax.axis_size(axis)
    pairs = [(source, (source + steps) % count) for source in range(count)]
    return lax.ppermute(value, axis, pairs)


def decay_rates(layer):
    depth_front = (layer - jnp.arange(layer)).astype(jnp.float32) / layer
    depth_back = (jnp.arange(layer) + 1).astype(jnp.float32) / layer
    depth = jnp.stack([depth_front, depth_back])
    return jnp.exp(-pml_rate * depth**3)


def forward_z(values, edge):
    return jnp.concatenate([values[1:], edge], 0) - values


def forward_x(values, edge):
    return jnp.concatenate([values[:, 1:], edge], 1) - values


def forward_y(values, edge):
    return jnp.concatenate([values[:, :, 1:], edge[:, :, None]], 2) - values


def backward_z(values, edge):
    return values - jnp.concatenate([edge, values[:-1]], 0)


def backward_x(values, edge):
    return values - jnp.concatenate([edge, values[:, :-1]], 1)


def backward_y(values, edge):
    return values - jnp.concatenate([edge[:, :, None], values[:, :, :-1]], 2)


def edge_layer(active_end, state_old, boundary, depth_rates):

    def renew():
        renewed = (
            depth_rates[:, None, None] * state_old + (depth_rates - 1.0)[:, None, None] * boundary
        )
        return (renewed, boundary + renewed)

    def keep():
        return (state_old, boundary)

    return lax.cond(active_end, renew, keep)


def absorb(derivative, state_pair, rates, at_front, at_back, back_start):
    layer = state_pair.shape[1]
    front_state, leading = edge_layer(at_front, state_pair[0], derivative[:layer], rates[0])
    back_state, trailing = edge_layer(
        at_back, state_pair[1], derivative[back_start : back_start + layer], rates[1]
    )
    merged = jnp.concatenate(
        [leading, derivative[layer:back_start], trailing, derivative[back_start + layer :]], 0
    )
    return (merged, jnp.stack([front_state, back_state]))


def next_planes(electric):
    return from_behind(electric[0:2, 0:1], "gz", -1)


def shards(electric, magnetic, aux_state, material, kerr_strength):
    planes = electric.shape[1]
    position = lax.axis_index("gz")
    at_front = position == 0
    at_back = position == lax.axis_size("gz") - 1
    rates = decay_rates(PML)
    core = material == 1
    eps_lin = jnp.where(core, eps_core, eps_clad).astype(jnp.float32)
    kerr_cell = jnp.where(core, kerr_strength[1], kerr_strength[0])
    aux_list = [aux_state[0], aux_state[1], aux_state[2], aux_state[3]]
    back_start = planes - PML
    e_next = next_planes(electric)
    for step_index in range(STEPS):
        elec_x, elec_y, elec_z = (electric[0], electric[1], electric[2])
        magn_x, magn_y, magn_z = (magnetic[0], magnetic[1], magnetic[2])
        next_cols = shifted(electric[1:3, :, 0:1, :], "gx", -1)
        next_rows = shifted(jnp.stack([elec_x[:, :, 0], elec_z[:, :, 0]]), "gy", -1)
        slope_y, aux_list[0] = absorb(
            forward_z(elec_y, e_next[1]), aux_list[0], rates, at_front, at_back, back_start
        )
        slope_x, aux_list[1] = absorb(
            forward_z(elec_x, e_next[0]), aux_list[1], rates, at_front, at_back, back_start
        )
        magn_x = magn_x - courant * (forward_y(elec_z, next_rows[1]) - slope_y)
        magn_y = magn_y - courant * (slope_x - forward_x(elec_z, next_cols[1]))
        magn_z = magn_z - courant * (
            forward_x(elec_y, next_cols[0]) - forward_y(elec_x, next_rows[0])
        )
        magnetic = jnp.stack([magn_x, magn_y, magn_z])
        h_prev = from_behind(magnetic[0:2, planes - 1 :], "gz", 1)
        prev_cols = shifted(magnetic[1:3, :, -1:, :], "gx", 1)
        prev_rows = shifted(jnp.stack([magn_x[:, :, -1], magn_z[:, :, -1]]), "gy", 1)
        factor = courant / (
            eps_lin + kerr_cell * (elec_x * elec_x + elec_y * elec_y + elec_z * elec_z)
        )
        slope_hy, aux_list[2] = absorb(
            backward_z(magn_y, h_prev[1]), aux_list[2], rates, at_front, at_back, back_start
        )
        slope_hx, aux_list[3] = absorb(
            backward_z(magn_x, h_prev[0]), aux_list[3], rates, at_front, at_back, back_start
        )
        new_x = elec_x + factor * (backward_y(magn_z, prev_rows[1]) - slope_hy)
        new_y = elec_y + factor * (slope_hx - backward_x(magn_z, prev_cols[1]))
        new_z = elec_z + factor * (
            backward_x(magn_y, prev_cols[0]) - backward_y(magn_x, prev_rows[0])
        )
        fields = jnp.stack([new_x, new_y, new_z, magn_x, magn_y, magn_z])
        arrived = from_behind(fields[:, 0:1], "gz", -1)
        fields = jnp.concatenate([fields[:, 1:], arrived], 1)
        if step_index + 1 < STEPS:
            e_next = next_planes(fields[0:3])
        electric = fields[0:3]
        magnetic = fields[3:6]
    return (electric, magnetic)


def solution(mesh):
    in_specs = (
        P(None, "gz", "gx", "gy"),
        P(None, "gz", "gx", "gy"),
        P(None, None, None, "gx", "gy"),
        P("gx", "gy"),
        P(),
    )
    out_specs = (P(None, "gz", "gx", "gy"), P(None, "gz", "gx", "gy"))
    return jax.shard_map(shards, mesh=mesh, in_specs=in_specs, out_specs=out_specs, check_vma=False)
```

profile of v0, /device:TPU:56, one launch (start us, length us, event | category | flops | bytes accessed | tf_op | source)
XLA Modules:
  0.0 166.2 jit_solution(13631250621016320580)
XLA Ops:
  2.2 8.4 %collective-permute-start.2 = (f32[2,1,16,128]{3,2,1,0:T(8,128)S(1)}, f32[2,1,16,128]{3,2,1,0:T(8,128)S(1)}, u32[]{:S(2)}, u32[]{:S(2)}) collective-permute-start(f32[2,1,16,128]{3,2,1,0:T(8,128)S(1)} %slice.793), channel_id=1, source_target_pairs={{16,0},{32,16},{48,32},{64,48},{80,64},{96,80},{112,96},{128,112},... | collective-permute-start | bytes 49160 | tf_op jit(solution)/shard_map/ppermute | solution.py:19
  10.6 1.6 collective-permute-start
  23.5 1.9 %collective-permute-start.4 = (f32[2,1,16,128]{3,2,1,0:T(8,128)S(1)}, f32[2,1,16,128]{3,2,1,0:T(8,128)S(1)}, u32[]{:S(2)}, u32[]{:S(2)}) collective-permute-start(f32[2,1,16,128]{3,2,1,0:T(8,128)S(1)} %pad_maximum_fusion.14), channel_id=1, source_target_pairs={{0,16},{16,32},{32,48},{48,64},{64,80},{80,96},{96,112},{112,128},... | collective-permute-start | bytes 49160 | tf_op jit(solution)/shard_map/ppermute | solution.py:19
  26.4 5.7 %collective-permute-done.4 = f32[2,1,16,128]{3,2,1,0:T(8,128)S(1)} collective-permute-done((f32[2,1,16,128]{3,2,1,0:T(8,128)S(1)}, f32[2,1,16,128]{3,2,1,0:T(8,128)S(1)}, u32[]{:S(2)}, u32[]{:S(2)}) %collective-permute-start.4) | collective-permute-done | bytes 16416 | tf_op jit(solution)/shard_map/ppermute | solution.py:19
  36.9 2.1 %collective-permute-done.5 = f32[2,16,1,128]{3,2,1,0:T(1,128)S(1)} collective-permute-done((f32[2,16,1,128]{3,2,1,0:T(1,128)S(1)}, f32[2,16,1,128]{3,2,1,0:T(1,128)S(1)}, u32[]{:S(2)}, u32[]{:S(2)}) %collective-permute-start.5) | collective-permute-done | bytes 16416 | tf_op jit(solution)/shard_map/ppermute | solution.py:25
  39.1 2.1 %collective-permute-start.9 = (f32[2,1,16,128]{3,2,1,0:T(8,128)S(1)}, f32[2,1,16,128]{3,2,1,0:T(8,128)S(1)}, u32[]{:S(2)}, u32[]{:S(2)}) collective-permute-start(f32[2,1,16,128]{3,2,1,0:T(8,128)S(1)} %pad_maximum_fusion.12), channel_id=1, source_target_pairs={{16,0},{32,16},{48,32},{64,48},{80,64},{96,80},{112,96},{128,112},... | collective-permute-start | bytes 49160 | tf_op jit(solution)/shard_map/ppermute | solution.py:19
  41.5 3.0 %collective-permute-start.6 = (f32[6,1,16,128]{3,2,1,0:T(8,128)S(1)}, f32[6,1,16,128]{3,2,1,0:T(8,128)S(1)}, u32[]{:S(2)}, u32[]{:S(2)}) collective-permute-start(f32[6,1,16,128]{3,2,1,0:T(8,128)S(1)} %slice.1023), channel_id=1, source_target_pairs={{16,0},{32,16},{48,32},{64,48},{80,64},{96,80},{112,96},{128,112},... | collective-permute-start | bytes 147464 | tf_op jit(solution)/shard_map/ppermute | solution.py:19
  45.8 2.8 %collective-permute-done.6 = f32[6,1,16,128]{3,2,1,0:T(8,128)S(1)} collective-permute-done((f32[6,1,16,128]{3,2,1,0:T(8,128)S(1)}, f32[6,1,16,128]{3,2,1,0:T(8,128)S(1)}, u32[]{:S(2)}, u32[]{:S(2)}) %collective-permute-start.6) | collective-permute-done | bytes 49184 | tf_op jit(solution)/shard_map/ppermute | solution.py:19
  51.4 1.6 collective-permute-done.8
  59.9 6.0 %collective-permute-start.11 = (f32[2,1,16,128]{3,2,1,0:T(8,128)S(1)}, f32[2,1,16,128]{3,2,1,0:T(8,128)S(1)}, u32[]{:S(2)}, u32[]{:S(2)}) collective-permute-start(f32[2,1,16,128]{3,2,1,0:T(8,128)S(1)} %pad_maximum_fusion.11), channel_id=1, source_target_pairs={{0,16},{16,32},{32,48},{48,64},{64,80},{80,96},{96,112},{112,128},... | collective-permute-start | bytes 49160 | tf_op jit(solution)/shard_map/ppermute | solution.py:19
  71.2 1.8 %constant_dynamic-update-slice_fusion.9 = (f32[6,16,16,128]{3,2,1,0:T(8,128)S(1)}, f32[1,16,16,128]{3,2,1,0:T(8,128)}, f32[1,16,16,128]{3,2,1,0:T(8,128)S(1)}) fusion(f32[1,16,16,128]{3,2,1,0:T(8,128)S(1)} %get-tuple-element.1325, f32[1,8,16,128]{3,2,1,0:T(8,128)S(1)} %bitcast.411, f32[1,8,16,128]{3,2,1,0:T(8,128)S(1)} %bitcast.406, ...), kind=kLoop, calls=%fused_computation.378 | loop fusion | flops 720895 | bytes 2113536
  75.3 2.1 %collective-permute-done.12 = f32[2,16,1,128]{3,2,1,0:T(1,128)S(1)} collective-permute-done((f32[2,16,1,128]{3,2,1,0:T(1,128)S(1)}, f32[2,16,1,128]{3,2,1,0:T(1,128)S(1)}, u32[]{:S(2)}, u32[]{:S(2)}) %collective-permute-start.12) | collective-permute-done | bytes 16416 | tf_op jit(solution)/shard_map/ppermute | solution.py:25
  78.3 3.0 %collective-permute-start.16 = (f32[2,1,16,128]{3,2,1,0:T(8,128)S(1)}, f32[2,1,16,128]{3,2,1,0:T(8,128)S(1)}, u32[]{:S(2)}, u32[]{:S(2)}) collective-permute-start(f32[2,1,16,128]{3,2,1,0:T(8,128)S(1)} %pad_maximum_fusion.9), channel_id=1, source_target_pairs={{16,0},{32,16},{48,32},{64,48},{80,64},{96,80},{112,96},{128,112},... | collective-permute-start | bytes 49160 | tf_op jit(solution)/shard_map/ppermute | solution.py:19
  81.6 4.0 %collective-permute-start.13 = (f32[6,1,16,128]{3,2,1,0:T(8,128)S(1)}, f32[6,1,16,128]{3,2,1,0:T(8,128)S(1)}, u32[]{:S(2)}, u32[]{:S(2)}) collective-permute-start(f32[6,1,16,128]{3,2,1,0:T(8,128)S(1)} %slice.1075), channel_id=1, source_target_pairs={{16,0},{32,16},{48,32},{64,48},{80,64},{96,80},{112,96},{128,112},... | collective-permute-start | bytes 147464 | tf_op jit(solution)/shard_map/ppermute | solution.py:19
  85.7 2.9 %collective-permute-done.13 = f32[6,1,16,128]{3,2,1,0:T(8,128)S(1)} collective-permute-done((f32[6,1,16,128]{3,2,1,0:T(8,128)S(1)}, f32[6,1,16,128]{3,2,1,0:T(8,128)S(1)}, u32[]{:S(2)}, u32[]{:S(2)}) %collective-permute-start.13) | collective-permute-done | bytes 49184 | tf_op jit(solution)/shard_map/ppermute | solution.py:19
  89.2 1.6 collective-permute-start.15
  94.4 1.3 fusion.197
  97.7 1.6 collective-permute-start.17
  100.8 5.2 %collective-permute-start.18 = (f32[2,1,16,128]{3,2,1,0:T(8,128)S(1)}, f32[2,1,16,128]{3,2,1,0:T(8,128)S(1)}, u32[]{:S(2)}, u32[]{:S(2)}) collective-permute-start(f32[2,1,16,128]{3,2,1,0:T(8,128)S(1)} %pad_maximum_fusion.8), channel_id=1, source_target_pairs={{0,16},{16,32},{32,48},{48,64},{64,80},{80,96},{96,112},{112,128},... | collective-permute-start | bytes 49160 | tf_op jit(solution)/shard_map/ppermute | solution.py:19
  107.7 1.9 %collective-permute-done.18 = f32[2,1,16,128]{3,2,1,0:T(8,128)S(1)} collective-permute-done((f32[2,1,16,128]{3,2,1,0:T(8,128)S(1)}, f32[2,1,16,128]{3,2,1,0:T(8,128)S(1)}, u32[]{:S(2)}, u32[]{:S(2)}) %collective-permute-start.18) | collective-permute-done | bytes 16416 | tf_op jit(solution)/shard_map/ppermute | solution.py:19
  112.3 1.8 %constant_dynamic-update-slice_fusion.14 = (f32[6,16,16,128]{3,2,1,0:T(8,128)S(1)}, f32[1,16,16,128]{3,2,1,0:T(8,128)}, f32[1,16,16,128]{3,2,1,0:T(8,128)S(1)}) fusion(f32[1,16,16,128]{3,2,1,0:T(8,128)S(1)} %get-tuple-element.1321, f32[1,8,16,128]{3,2,1,0:T(8,128)S(1)} %bitcast.413, f32[1,8,16,128]{3,2,1,0:T(8,128)S(1)} %bitcast.408, ...), kind=kLoop, calls=%fused_computation.383 | loop fusion | flops 720895 | bytes 2113536
  116.4 2.1 %collective-permute-done.19 = f32[2,16,1,128]{3,2,1,0:T(1,128)S(1)} collective-permute-done((f32[2,16,1,128]{3,2,1,0:T(1,128)S(1)}, f32[2,16,1,128]{3,2,1,0:T(1,128)S(1)}, u32[]{:S(2)}, u32[]{:S(2)}) %collective-permute-start.19) | collective-permute-done | bytes 16416 | tf_op jit(solution)/shard_map/ppermute | solution.py:25
  119.4 3.5 %collective-permute-start.23 = (f32[2,1,16,128]{3,2,1,0:T(8,128)S(1)}, f32[2,1,16,128]{3,2,1,0:T(8,128)S(1)}, u32[]{:S(2)}, u32[]{:S(2)}) collective-permute-start(f32[2,1,16,128]{3,2,1,0:T(8,128)S(1)} %pad_maximum_fusion.6), channel_id=1, source_target_pairs={{16,0},{32,16},{48,32},{64,48},{80,64},{96,80},{112,96},{128,112},... | collective-permute-start | bytes 49160 | tf_op jit(solution)/shard_map/ppermute | solution.py:19
  123.2 4.4 %collective-permute-start.20 = (f32[6,1,16,128]{3,2,1,0:T(8,128)S(1)}, f32[6,1,16,128]{3,2,1,0:T(8,128)S(1)}, u32[]{:S(2)}, u32[]{:S(2)}) collective-permute-start(f32[6,1,16,128]{3,2,1,0:T(8,128)S(1)} %slice.1127), channel_id=1, source_target_pairs={{16,0},{32,16},{48,32},{64,48},{80,64},{96,80},{112,96},{128,112},... | collective-permute-start | bytes 147464 | tf_op jit(solution)/shard_map/ppermute | solution.py:19
  127.6 2.6 %collective-permute-done.20 = f32[6,1,16,128]{3,2,1,0:T(8,128)S(1)} collective-permute-done((f32[6,1,16,128]{3,2,1,0:T(8,128)S(1)}, f32[6,1,16,128]{3,2,1,0:T(8,128)S(1)}, u32[]{:S(2)}, u32[]{:S(2)}) %collective-permute-start.20) | collective-permute-done | bytes 49184 | tf_op jit(solution)/shard_map/ppermute | solution.py:19
  131.1 1.7 %collective-permute-start.22 = (f32[2,16,16]{2,1,0:T(8,128)S(1)}, f32[2,16,16]{2,1,0:T(8,128)S(1)}, u32[]{:S(2)}, u32[]{:S(2)}) collective-permute-start(f32[2,16,16]{2,1,0:T(8,128)S(1)} %pad_maximum_fusion.21), channel_id=1, source_target_pairs={{0,1},{1,0},{2,3},{3,2},{4,5},{5,4},{6,7},{7,6},{8,9},{9,8},{10,11... | collective-permute-start | bytes 6152 | tf_op jit(solution)/shard_map/ppermute | solution.py:25
  138.1 1.7 %collective-permute-start.24 = (f32[2,16,16]{2,1,0:T(8,128)S(1)}, f32[2,16,16]{2,1,0:T(8,128)S(1)}, u32[]{:S(2)}, u32[]{:S(2)}) collective-permute-start(f32[2,16,16]{2,1,0:T(8,128)S(1)} %pad_maximum_fusion.22), channel_id=1, source_target_pairs={{0,1},{1,0},{2,3},{3,2},{4,5},{5,4},{6,7},{7,6},{8,9},{9,8},{10,11... | collective-permute-start | bytes 6152 | tf_op jit(solution)/shard_map/ppermute | solution.py:25
  140.6 3.0 %collective-permute-start.25 = (f32[2,1,16,128]{3,2,1,0:T(8,128)S(1)}, f32[2,1,16,128]{3,2,1,0:T(8,128)S(1)}, u32[]{:S(2)}, u32[]{:S(2)}) collective-permute-start(f32[2,1,16,128]{3,2,1,0:T(8,128)S(1)} %pad_maximum_fusion.5), channel_id=1, source_target_pairs={{0,16},{16,32},{32,48},{48,64},{64,80},{80,96},{96,112},{112,128},... | collective-permute-start | bytes 49160 | tf_op jit(solution)/shard_map/ppermute | solution.py:19
  144.6 4.6 %collective-permute-done.25 = f32[2,1,16,128]{3,2,1,0:T(8,128)S(1)} collective-permute-done((f32[2,1,16,128]{3,2,1,0:T(8,128)S(1)}, f32[2,1,16,128]{3,2,1,0:T(8,128)S(1)}, u32[]{:S(2)}, u32[]{:S(2)}) %collective-permute-start.25) | collective-permute-done | bytes 16416 | tf_op jit(solution)/shard_map/ppermute | solution.py:19
  155.4 2.1 %collective-permute-done.26 = f32[2,16,1,128]{3,2,1,0:T(1,128)S(1)} collective-permute-done((f32[2,16,1,128]{3,2,1,0:T(1,128)S(1)}, f32[2,16,1,128]{3,2,1,0:T(1,128)S(1)}, u32[]{:S(2)}, u32[]{:S(2)}) %collective-permute-start.26) | collective-permute-done | bytes 16416 | tf_op jit(solution)/shard_map/ppermute | solution.py:25
  157.8 4.2 %collective-permute-start.27 = (f32[6,1,16,128]{3,2,1,0:T(8,128)S(1)}, f32[6,1,16,128]{3,2,1,0:T(8,128)S(1)}, u32[]{:S(2)}, u32[]{:S(2)}) collective-permute-start(f32[6,1,16,128]{3,2,1,0:T(8,128)S(1)} %slice.1179), channel_id=1, source_target_pairs={{16,0},{32,16},{48,32},{64,48},{80,64},{96,80},{112,96},{128,112},... | collective-permute-start | bytes 147464 | tf_op jit(solution)/shard_map/ppermute | solution.py:19
  162.1 3.1 %collective-permute-done.27 = f32[6,1,16,128]{3,2,1,0:T(8,128)S(1)} collective-permute-done((f32[6,1,16,128]{3,2,1,0:T(8,128)S(1)}, f32[6,1,16,128]{3,2,1,0:T(8,128)S(1)}, u32[]{:S(2)}, u32[]{:S(2)}) %collective-permute-start.27) | collective-permute-done | bytes 49184 | tf_op jit(solution)/shard_map/ppermute | solution.py:19
  (411 shorter events, 68.0 us)
Async XLA Ops:
  2.0 15.3 %collective-permute-start.1 = (f32[2,16,16]{2,1,0:T(8,128)S(1)}, f32[2,16,16]{2,1,0:T(8,128)S(1)}, u32[]{:S(2)}, u32[]{:S(2)}) collective-permute-start(f32[2,16,16]{2,1,0:T(8,128)S(1)} %pad_maximum_fusion.15), channel_id=1, source_target_pairs={{0,1},{1,0},{2,3},{3,2},{4,5},{5,4},{6,7},{7,6},{8,9},{9,8},{10,11... | collective-permute-start | bytes 6152 | tf_op jit(solution)/shard_map/ppermute | solution.py:25
  2.2 15.8 %collective-permute-start.2 = (f32[2,1,16,128]{3,2,1,0:T(8,128)S(1)}, f32[2,1,16,128]{3,2,1,0:T(8,128)S(1)}, u32[]{:S(2)}, u32[]{:S(2)}) collective-permute-start(f32[2,1,16,128]{3,2,1,0:T(8,128)S(1)} %slice.793), channel_id=1, source_target_pairs={{16,0},{32,16},{48,32},{64,48},{80,64},{96,80},{112,96},{128,112},... | collective-permute-start | bytes 49160 | tf_op jit(solution)/shard_map/ppermute | solution.py:19
  10.6 7.6 %collective-permute-start = (f32[2,16,1,128]{3,2,1,0:T(1,128)S(1)}, f32[2,16,1,128]{3,2,1,0:T(1,128)S(1)}, u32[]{:S(2)}, u32[]{:S(2)}) collective-permute-start(f32[2,16,1,128]{3,2,1,0:T(1,128)S(1)} %slice.781), channel_id=1, source_target_pairs={{0,14},{2,0},{4,2},{6,4},{8,6},{10,8},{12,10},{14,12},{1,15},{3,1}... | collective-permute-start | bytes 49160 | tf_op jit(solution)/shard_map/ppermute | solution.py:25
  17.2 15.5 %copy-start.29 = (f32[1,8]{1,0:T(1,128)}, f32[1,8]{1,0:T(1,128)S(1)}, u32[]{:S(2)}) copy-start(f32[1,8]{1,0:T(1,128)S(1)} %get-tuple-element.1474) | copy-start | bytes 100
  17.2 15.5 %copy-start.61 = (f32[8]{0:T(128)}, f32[8]{0:T(128)S(1)}, u32[]{:S(2)}) copy-start(f32[8]{0:T(128)S(1)} %get-tuple-element.1473) | copy-start | bytes 100
  17.2 15.6 %copy-start.19 = (f32[1,8]{1,0:T(1,128)}, f32[1,8]{1,0:T(1,128)S(1)}, u32[]{:S(2)}) copy-start(f32[1,8]{1,0:T(1,128)S(1)} %get-tuple-element.1475) | copy-start | bytes 100
  17.3 15.6 %copy-start.51 = (f32[8]{0:T(128)}, f32[8]{0:T(128)S(1)}, u32[]{:S(2)}) copy-start(f32[8]{0:T(128)S(1)} %get-tuple-element.1472) | copy-start | bytes 100
  21.1 4.3 %collective-permute-start.3 = (f32[2,16,16]{2,1,0:T(8,128)S(1)}, f32[2,16,16]{2,1,0:T(8,128)S(1)}, u32[]{:S(2)}, u32[]{:S(2)}) collective-permute-start(f32[2,16,16]{2,1,0:T(8,128)S(1)} %pad_maximum_fusion.16), channel_id=1, source_target_pairs={{0,1},{1,0},{2,3},{3,2},{4,5},{5,4},{6,7},{7,6},{8,9},{9,8},{10,11... | collective-permute-start | bytes 6152 | tf_op jit(solution)/shard_map/ppermute | solution.py:25
  23.5 8.6 %collective-permute-start.4 = (f32[2,1,16,128]{3,2,1,0:T(8,128)S(1)}, f32[2,1,16,128]{3,2,1,0:T(8,128)S(1)}, u32[]{:S(2)}, u32[]{:S(2)}) collective-permute-start(f32[2,1,16,128]{3,2,1,0:T(8,128)S(1)} %pad_maximum_fusion.14), channel_id=1, source_target_pairs={{0,16},{16,32},{32,48},{48,64},{64,80},{80,96},{96,112},{112,128},... | collective-permute-start | bytes 49160 | tf_op jit(solution)/shard_map/ppermute | solution.py:19
  34.6 4.4 %collective-permute-start.5 = (f32[2,16,1,128]{3,2,1,0:T(1,128)S(1)}, f32[2,16,1,128]{3,2,1,0:T(1,128)S(1)}, u32[]{:S(2)}, u32[]{:S(2)}) collective-permute-start(f32[2,16,1,128]{3,2,1,0:T(1,128)S(1)} %pad_maximum_fusion.13), channel_id=1, source_target_pairs={{0,2},{2,4},{4,6},{6,8},{8,10},{10,12},{12,14},{14,0},{1,3},{3,5},... | collective-permute-start | bytes 49160 | tf_op jit(solution)/shard_map/ppermute | solution.py:25
  39.1 6.7 %collective-permute-start.9 = (f32[2,1,16,128]{3,2,1,0:T(8,128)S(1)}, f32[2,1,16,128]{3,2,1,0:T(8,128)S(1)}, u32[]{:S(2)}, u32[]{:S(2)}) collective-permute-start(f32[2,1,16,128]{3,2,1,0:T(8,128)S(1)} %pad_maximum_fusion.12), channel_id=1, source_target_pairs={{16,0},{32,16},{48,32},{64,48},{80,64},{96,80},{112,96},{128,112},... | collective-permute-start | bytes 49160 | tf_op jit(solution)/shard_map/ppermute | solution.py:19
  41.5 7.2 %collective-permute-start.6 = (f32[6,1,16,128]{3,2,1,0:T(8,128)S(1)}, f32[6,1,16,128]{3,2,1,0:T(8,128)S(1)}, u32[]{:S(2)}, u32[]{:S(2)}) collective-permute-start(f32[6,1,16,128]{3,2,1,0:T(8,128)S(1)} %slice.1023), channel_id=1, source_target_pairs={{16,0},{32,16},{48,32},{64,48},{80,64},{96,80},{112,96},{128,112},... | collective-permute-start | bytes 147464 | tf_op jit(solution)/shard_map/ppermute | solution.py:19
  49.2 3.8 %collective-permute-start.8 = (f32[2,16,16]{2,1,0:T(8,128)S(1)}, f32[2,16,16]{2,1,0:T(8,128)S(1)}, u32[]{:S(2)}, u32[]{:S(2)}) collective-permute-start(f32[2,16,16]{2,1,0:T(8,128)S(1)} %pad_maximum_fusion.17), channel_id=1, source_target_pairs={{0,1},{1,0},{2,3},{3,2},{4,5},{5,4},{6,7},{7,6},{8,9},{9,8},{10,11... | collective-permute-start | bytes 6152 | tf_op jit(solution)/shard_map/ppermute | solution.py:25
  50.7 3.7 %collective-permute-start.7 = (f32[2,16,1,128]{3,1,2,0:T(8,128)}, f32[2,16,1,128]{3,1,2,0:T(8,128)}, u32[]{:S(2)}, u32[]{:S(2)}) collective-permute-start(f32[2,16,1,128]{3,1,2,0:T(8,128)} %bitcast.211), channel_id=1, source_target_pairs={{0,14},{2,0},{4,2},{6,4},{8,6},{10,8},{12,10},{14,12},{1,15},{3,1}... | collective-permute-start | bytes 49160 | tf_op jit(solution)/shard_map/ppermute | solution.py:25
  57.6 8.3 %collective-permute-start.10 = (f32[2,16,16]{2,1,0:T(8,128)S(1)}, f32[2,16,16]{2,1,0:T(8,128)S(1)}, u32[]{:S(2)}, u32[]{:S(2)}) collective-permute-start(f32[2,16,16]{2,1,0:T(8,128)S(1)} %pad_maximum_fusion.18), channel_id=1, source_target_pairs={{0,1},{1,0},{2,3},{3,2},{4,5},{5,4},{6,7},{7,6},{8,9},{9,8},{10,11... | collective-permute-start | bytes 6152 | tf_op jit(solution)/shard_map/ppermute | solution.py:25
  59.9 8.6 %collective-permute-start.11 = (f32[2,1,16,128]{3,2,1,0:T(8,128)S(1)}, f32[2,1,16,128]{3,2,1,0:T(8,128)S(1)}, u32[]{:S(2)}, u32[]{:S(2)}) collective-permute-start(f32[2,1,16,128]{3,2,1,0:T(8,128)S(1)} %pad_maximum_fusion.11), channel_id=1, source_target_pairs={{0,16},{16,32},{32,48},{48,64},{64,80},{80,96},{96,112},{112,128},... | collective-permute-start | bytes 49160 | tf_op jit(solution)/shard_map/ppermute | solution.py:19
  73.0 4.4 %collective-permute-start.12 = (f32[2,16,1,128]{3,2,1,0:T(1,128)S(1)}, f32[2,16,1,128]{3,2,1,0:T(1,128)S(1)}, u32[]{:S(2)}, u32[]{:S(2)}) collective-permute-start(f32[2,16,1,128]{3,2,1,0:T(1,128)S(1)} %pad_maximum_fusion.10), channel_id=1, source_target_pairs={{0,2},{2,4},{4,6},{6,8},{8,10},{10,12},{12,14},{14,0},{1,3},{3,5},... | collective-permute-start | bytes 49160 | tf_op jit(solution)/shard_map/ppermute | solution.py:25
  78.3 7.4 %collective-permute-start.16 = (f32[2,1,16,128]{3,2,1,0:T(8,128)S(1)}, f32[2,1,16,128]{3,2,1,0:T(8,128)S(1)}, u32[]{:S(2)}, u32[]{:S(2)}) collective-permute-start(f32[2,1,16,128]{3,2,1,0:T(8,128)S(1)} %pad_maximum_fusion.9), channel_id=1, source_target_pairs={{16,0},{32,16},{48,32},{64,48},{80,64},{96,80},{112,96},{128,112},... | collective-permute-start | bytes 49160 | tf_op jit(solution)/shard_map/ppermute | solution.py:19
  81.6 7.0 %collective-permute-start.13 = (f32[6,1,16,128]{3,2,1,0:T(8,128)S(1)}, f32[6,1,16,128]{3,2,1,0:T(8,128)S(1)}, u32[]{:S(2)}, u32[]{:S(2)}) collective-permute-start(f32[6,1,16,128]{3,2,1,0:T(8,128)S(1)} %slice.1075), channel_id=1, source_target_pairs={{16,0},{32,16},{48,32},{64,48},{80,64},{96,80},{112,96},{128,112},... | collective-permute-start | bytes 147464 | tf_op jit(solution)/shard_map/ppermute | solution.py:19
  89.2 3.8 %collective-permute-start.15 = (f32[2,16,16]{2,1,0:T(8,128)S(1)}, f32[2,16,16]{2,1,0:T(8,128)S(1)}, u32[]{:S(2)}, u32[]{:S(2)}) collective-permute-start(f32[2,16,16]{2,1,0:T(8,128)S(1)} %pad_maximum_fusion.19), channel_id=1, source_target_pairs={{0,1},{1,0},{2,3},{3,2},{4,5},{5,4},{6,7},{7,6},{8,9},{9,8},{10,11... | collective-permute-start | bytes 6152 | tf_op jit(solution)/shard_map/ppermute | solution.py:25
  91.5 2.9 %collective-permute-start.14 = (f32[2,16,1,128]{3,2,1,0:T(1,128)}, f32[2,16,1,128]{3,2,1,0:T(1,128)}, u32[]{:S(2)}, u32[]{:S(2)}) collective-permute-start(f32[2,16,1,128]{3,2,1,0:T(1,128)} %fusion.131), channel_id=1, source_target_pairs={{0,14},{2,0},{4,2},{6,4},{8,6},{10,8},{12,10},{14,12},{1,15},{3,1}... | collective-permute-start | bytes 49160 | tf_op jit(solution)/shard_map/ppermute | solution.py:25
  97.7 8.3 %collective-permute-start.17 = (f32[2,16,16]{2,1,0:T(8,128)S(1)}, f32[2,16,16]{2,1,0:T(8,128)S(1)}, u32[]{:S(2)}, u32[]{:S(2)}) collective-permute-start(f32[2,16,16]{2,1,0:T(8,128)S(1)} %pad_maximum_fusion.20), channel_id=1, source_target_pairs={{0,1},{1,0},{2,3},{3,2},{4,5},{5,4},{6,7},{7,6},{8,9},{9,8},{10,11... | collective-permute-start | bytes 6152 | tf_op jit(solution)/shard_map/ppermute | solution.py:25
  100.8 8.8 %collective-permute-start.18 = (f32[2,1,16,128]{3,2,1,0:T(8,128)S(1)}, f32[2,1,16,128]{3,2,1,0:T(8,128)S(1)}, u32[]{:S(2)}, u32[]{:S(2)}) collective-permute-start(f32[2,1,16,128]{3,2,1,0:T(8,128)S(1)} %pad_maximum_fusion.8), channel_id=1, source_target_pairs={{0,16},{16,32},{32,48},{48,64},{64,80},{80,96},{96,112},{112,128},... | collective-permute-start | bytes 49160 | tf_op jit(solution)/shard_map/ppermute | solution.py:19
  114.1 4.4 %collective-permute-start.19 = (f32[2,16,1,128]{3,2,1,0:T(1,128)S(1)}, f32[2,16,1,128]{3,2,1,0:T(1,128)S(1)}, u32[]{:S(2)}, u32[]{:S(2)}) collective-permute-start(f32[2,16,1,128]{3,2,1,0:T(1,128)S(1)} %pad_maximum_fusion.7), channel_id=1, source_target_pairs={{0,2},{2,4},{4,6},{6,8},{8,10},{10,12},{12,14},{14,0},{1,3},{3,5},... | collective-permute-start | bytes 49160 | tf_op jit(solution)/shard_map/ppermute | solution.py:25
  119.4 8.2 %collective-permute-start.23 = (f32[2,1,16,128]{3,2,1,0:T(8,128)S(1)}, f32[2,1,16,128]{3,2,1,0:T(8,128)S(1)}, u32[]{:S(2)}, u32[]{:S(2)}) collective-permute-start(f32[2,1,16,128]{3,2,1,0:T(8,128)S(1)} %pad_maximum_fusion.6), channel_id=1, source_target_pairs={{16,0},{32,16},{48,32},{64,48},{80,64},{96,80},{112,96},{128,112},... | collective-permute-start | bytes 49160 | tf_op jit(solution)/shard_map/ppermute | solution.py:19
  123.2 7.0 %collective-permute-start.20 = (f32[6,1,16,128]{3,2,1,0:T(8,128)S(1)}, f32[6,1,16,128]{3,2,1,0:T(8,128)S(1)}, u32[]{:S(2)}, u32[]{:S(2)}) collective-permute-start(f32[6,1,16,128]{3,2,1,0:T(8,128)S(1)} %slice.1127), channel_id=1, source_target_pairs={{16,0},{32,16},{48,32},{64,48},{80,64},{96,80},{112,96},{128,112},... | collective-permute-start | bytes 147464 | tf_op jit(solution)/shard_map/ppermute | solution.py:19
  130.7 5.6 %collective-permute-start.21 = (f32[2,16,1,128]{3,1,2,0:T(8,128)S(1)}, f32[2,16,1,128]{3,1,2,0:T(8,128)S(1)}, u32[]{:S(2)}, u32[]{:S(2)}) collective-permute-start(f32[2,16,1,128]{3,1,2,0:T(8,128)S(1)} %bitcast.472), channel_id=1, source_target_pairs={{0,14},{2,0},{4,2},{6,4},{8,6},{10,8},{12,10},{14,12},{1,15},{3,1}... | collective-permute-start | bytes 49160 | tf_op jit(solution)/shard_map/ppermute | solution.py:25
  131.1 3.8 %collective-permute-start.22 = (f32[2,16,16]{2,1,0:T(8,128)S(1)}, f32[2,16,16]{2,1,0:T(8,128)S(1)}, u32[]{:S(2)}, u32[]{:S(2)}) collective-permute-start(f32[2,16,16]{2,1,0:T(8,128)S(1)} %pad_maximum_fusion.21), channel_id=1, source_target_pairs={{0,1},{1,0},{2,3},{3,2},{4,5},{5,4},{6,7},{7,6},{8,9},{9,8},{10,11... | collective-permute-start | bytes 6152 | tf_op jit(solution)/shard_map/ppermute | solution.py:25
  138.1 5.5 %collective-permute-start.24 = (f32[2,16,16]{2,1,0:T(8,128)S(1)}, f32[2,16,16]{2,1,0:T(8,128)S(1)}, u32[]{:S(2)}, u32[]{:S(2)}) collective-permute-start(f32[2,16,16]{2,1,0:T(8,128)S(1)} %pad_maximum_fusion.22), channel_id=1, source_target_pairs={{0,1},{1,0},{2,3},{3,2},{4,5},{5,4},{6,7},{7,6},{8,9},{9,8},{10,11... | collective-permute-start | bytes 6152 | tf_op jit(solution)/shard_map/ppermute | solution.py:25
  140.6 8.6 %collective-permute-start.25 = (f32[2,1,16,128]{3,2,1,0:T(8,128)S(1)}, f32[2,1,16,128]{3,2,1,0:T(8,128)S(1)}, u32[]{:S(2)}, u32[]{:S(2)}) collective-permute-start(f32[2,1,16,128]{3,2,1,0:T(8,128)S(1)} %pad_maximum_fusion.5), channel_id=1, source_target_pairs={{0,16},{16,32},{32,48},{48,64},{64,80},{80,96},{96,112},{112,128},... | collective-permute-start | bytes 49160 | tf_op jit(solution)/shard_map/ppermute | solution.py:19
  153.2 4.4 %collective-permute-start.26 = (f32[2,16,1,128]{3,2,1,0:T(1,128)S(1)}, f32[2,16,1,128]{3,2,1,0:T(1,128)S(1)}, u32[]{:S(2)}, u32[]{:S(2)}) collective-permute-start(f32[2,16,1,128]{3,2,1,0:T(1,128)S(1)} %pad_maximum_fusion.4), channel_id=1, source_target_pairs={{0,2},{2,4},{4,6},{6,8},{8,10},{10,12},{12,14},{14,0},{1,3},{3,5},... | collective-permute-start | bytes 49160 | tf_op jit(solution)/shard_map/ppermute | solution.py:25
  157.8 7.4 %collective-permute-start.27 = (f32[6,1,16,128]{3,2,1,0:T(8,128)S(1)}, f32[6,1,16,128]{3,2,1,0:T(8,128)S(1)}, u32[]{:S(2)}, u32[]{:S(2)}) collective-permute-start(f32[6,1,16,128]{3,2,1,0:T(8,128)S(1)} %slice.1179), channel_id=1, source_target_pairs={{16,0},{32,16},{48,32},{64,48},{80,64},{96,80},{112,96},{128,112},... | collective-permute-start | bytes 147464 | tf_op jit(solution)/shard_map/ppermute | solution.py:19
  (67 other events, 66.6 us)
where the time goes:
time: 168 us; the launch traced here: 166 us
  starting transfers between devices  60.9 us (36%)
  local copies, waits for them, and re-layouts  54 us (32%)
  waiting for transfers between devices  37 us (22%)
  other arithmetic  11.8 us (7%)
  between operations  2.26 us (1%)
    ppermute x12, starting transfers between devices, from_behind(): return lax.ppermute(shard, axis, pairs)  48.7 us
    ppermute x12, waiting for transfers between devices, from_behind(): return lax.ppermute(shard, axis, pairs)  25.9 us
    unnamed x154, local copies, waits for them, and re-layouts  24 us
    ppermute x16, starting transfers between devices, shifted(): return lax.ppermute(value, axis, pairs)  12.2 us
    ppermute x16, waiting for transfers between devices, shifted(): return lax.ppermute(value, axis, pairs)  11.1 us
    concatenate x20, local copies, waits for them, and re-layouts, backward_y(): return values - jnp.concatenate([edge[:, :, None], values[:, :, :-1]], 2)  7.99 us
    unnamed x12, other arithmetic  6.64 us
    concatenate x17, local copies, waits for them, and re-layouts, forward_y(): return jnp.concatenate([values[:, :, 1:], edge[:, :, None]], 2) - values  4.48 us
  transfers between devices with their start and end apart: 28, of which 16 were waited for; matrix products, arithmetic and copies ran while one was open for 12% of the time, Pallas kernels for 0%

commit v1 on v0

v1 whole, which is shorter than its diff:
```python
import functools

import jax
import jax.numpy as jnp
from jax import lax
from jax.experimental import pallas as pl
from jax.experimental.pallas import tpu as pltpu
from jax.sharding import PartitionSpec as P

PML = 8
STEPS = 4
HALO = 4
DEEP = 8
PLANES = 16
ROWS = 16
LANES = 128
TALL = ROWS + 2 * HALO
WIDE = 2 * LANES
FIELDS = 6
DEPTHS = (8, 8, 7, 7, 7, 7)
SENT = sum(DEPTHS)
OWN = FIELDS * PLANES
AUX = 4 * PML
MAT = OWN + AUX
TAKEN = MAT + 1
GROUPS = (TAKEN + 15) // 16
KEPT = 5

courant = 0.5
pml_rate = 3.0
eps_clad = 2.085
eps_core = 4.0

VMEM = pl.BlockSpec(memory_space=pltpu.VMEM)
SMEM = pl.BlockSpec(memory_space=pltpu.SMEM)
F32 = jnp.float32


def decay_rates(layer):
    depth_front = (layer - jnp.arange(layer)).astype(jnp.float32) / layer
    depth_back = (jnp.arange(layer) + 1).astype(jnp.float32) / layer
    depth = jnp.stack([depth_front, depth_back])
    return jnp.exp(-pml_rate * depth**3)


def sent_index(c, z):
    return sum(DEPTHS[:c]) + z


def call(body, out_shape, in_specs, scratch=(), **more):
    n_out = len(out_shape)
    more.setdefault("out_specs", [VMEM] * n_out)
    return pl.pallas_call(
        body,
        out_shape=[jax.ShapeDtypeStruct(s, F32) for s in out_shape],
        in_specs=in_specs,
        scratch_shapes=list(scratch),
        compiler_params=pltpu.CompilerParams(vmem_limit_bytes=40 * 1024 * 1024),
        **more,
    )


def pack_body(e, h, aux, mat, low, mid, high, zstrip, ystrip):
    lane = lax.broadcasted_iota(jnp.int32, (ROWS, LANES), 1) // 8

    def strip(tiles):
        out = jnp.zeros((ROWS, LANES), F32)
        for k, tile in enumerate(tiles):
            out = jnp.where(lane == k, pltpu.roll(tile, (8 * k + HALO) % LANES, 1), out)
        return out

    strips = []
    for c in range(FIELDS):
        src = e if c < 3 else h
        for z in range(DEPTHS[c]):
            plane = src[c % 3, z]
            at = sent_index(c, z)
            low[at] = plane[0:4]
            mid[at] = plane[4:12]
            high[at] = plane[12:16]
        made = strip([src[c % 3, z] for z in range(PLANES)])
        ystrip[c] = made
        strips.append(made)
    half = lane < 8
    for j in range(3):
        zstrip[j] = jnp.where(half, strips[2 * j], pltpu.roll(strips[2 * j + 1], 64, 1))
    for j in range(2):
        ystrip[FIELDS + j] = strip([aux[2 * j + k // PML, 0, k % PML] for k in range(16)])
    ystrip[FIELDS + 2] = strip([mat[...]])


def rows_body(e, h, aux, mat, ystrip, to_left, to_right):
    def put(at, tile):
        to_left[at] = tile[0:4]
        to_right[at] = tile[12:16]

    for c in range(FIELDS):
        src = e if c < 3 else h
        for z in range(PLANES):
            put(c * PLANES + z, src[c % 3, z])
    for a in range(4):
        for k in range(PML):
            put(OWN + a * PML + k, aux[a, 0, k])
    put(MAT, mat[...])
    for g in range(GROUPS):
        put(TAKEN + g, ystrip[g])


def forward(value, axis):
    return pltpu.roll(value, value.shape[axis] - 1, axis) - value


def backward(value, axis):
    return value - pltpu.roll(value, 1, axis)


def absorb(slope, state, index, k, rate):
    old = state[index, k]
    kept = rate * (slope + old)
    state[index, k] = kept - slope
    return kept


def magnetic_plane(f, p, layer=None):
    ex, ey, ez = f[0, p], f[1, p], f[2, p]
    slope_y = f[1, p + 1] - ey
    slope_x = f[0, p + 1] - ex
    if layer is not None:
        state, k, rate = layer
        slope_y = absorb(slope_y, state, 0, k, rate)
        slope_x = absorb(slope_x, state, 1, k, rate)
    hx = f[3, p] - courant * (forward(ez, 1) - slope_y)
    hy = f[4, p] - courant * (slope_x - forward(ez, 0))
    hz = f[5, p] - courant * (forward(ey, 0) - forward(ex, 1))
    f[3, p] = hx
    f[4, p] = hy
    f[5, p] = hz
    return ex, ey, ez, hx, hy, hz


def whole_plane(f, cell, p, layer=None):
    ex, ey, ez, hx, hy, hz = magnetic_plane(f, p, layer)
    factor = courant / (cell[0] + cell[1] * (ex * ex + ey * ey + ez * ez))
    slope_hy = hy - f[4, p - 1]
    slope_hx = hx - f[3, p - 1]
    if layer is not None:
        state, k, rate = layer
        slope_hy = absorb(slope_hy, state, 2, k, rate)
        slope_hx = absorb(slope_hx, state, 3, k, rate)
    f[0, p] = ex + factor * (backward(hz, 1) - slope_hy)
    f[1, p] = ey + factor * (slope_hx - backward(hz, 0))
    f[2, p] = ez + factor * (backward(hy, 0) - backward(hx, 1))


def loop(start, stop, body):
    lax.fori_loop(start, stop, lambda i, _: (body(i), 0)[1], 0)


def early_body(
    place, rates, kerr, e, h, aux, mat, ystrip, left, right,
    out_e, out_h, kept, cell, f, state,
):
    at_front = place[0] == 0
    at_back = place[0] == place[1] - 1

    def tall(own, above, below):
        return jnp.concatenate([above, own, below], 0)

    def stripe(g):
        return tall(ystrip[g], left[TAKEN + g], right[TAKEN + g])

    def fill(dst, own, at):
        dst[:, 0:LANES] = tall(own, left[at], right[at])

    for c in range(FIELDS):
        src = e if c < 3 else h
        packed = stripe(c)
        for z in range(PLANES):
            dst = f.at[c, z]
            fill(dst, src[c % 3, z], c * PLANES + z)
            dst[:, LANES:WIDE] = pltpu.roll(packed, (2 * LANES - 8 * z - HALO) % LANES, 1)

    packed = stripe(FIELDS + 2)
    flag_own = tall(mat[...], left[MAT], right[MAT])
    flag = jnp.concatenate([flag_own, pltpu.roll(packed, LANES - HALO, 1)], 1) == 1.0
    cell[0] = jnp.where(flag, eps_core, eps_clad)
    cell[1] = jnp.where(flag, kerr[1], kerr[0])

    @pl.when(at_front | at_back)
    def _():
        for j in range(2):
            packed = stripe(FIELDS + j)
            for k in range(16):
                a, z = 2 * j + k // PML, k % PML
                dst = state.at[a, z]
                fill(dst, aux[a, 0, z], OWN + a * PML + z)
                dst[:, LANES:WIDE] = pltpu.roll(packed, (2 * LANES - 8 * k - HALO) % LANES, 1)

    @pl.when(at_back)
    def _():
        for c in range(FIELDS):
            for z in range(STEPS):
                f[c, PLANES + z] = jnp.zeros((TALL, WIDE), F32)

    def step(s):
        last = jnp.where(at_back, PLANES - 2 + s, PLANES - 1 - s)
        layer_from = jnp.where(at_front, s, jnp.where(at_back, PLANES - PML + s - 1, last + 1))
        layer_to = jnp.where(at_front, s + PML - 1, last + 1)
        first = jnp.where(at_front, s - 1, PLANES - PML + s - 1)

        @pl.when(at_front)
        def _():
            magnetic_plane(f, s - 1, (state, 0, rates[0]))

        @pl.when(jnp.logical_not(at_front))
        def _():
            magnetic_plane(f, s - 1)

        def plain(p):
            whole_plane(f, cell, p)

        def layered(p):
            k = p - first
            whole_plane(f, cell, p, (state, k, rates[k]))

        loop(s, layer_from, plain)
        loop(layer_from, layer_to, layered)
        loop(layer_to, last + 1, plain)

    loop(1, STEPS + 1, step)

    def give(z):
        for c in range(3):
            out_e[c, z] = f[c, z + STEPS, HALO : HALO + ROWS, 0:LANES]
            out_h[c, z] = f[3 + c, z + STEPS, HALO : HALO + ROWS, 0:LANES]

    loop(0, PLANES // 2, give)

    @pl.when(at_back)
    def _():
        loop(PLANES // 2, PLANES, give)

    for c in range(FIELDS):
        for z in range(KEPT):
            kept[c, z] = f[c, PLANES - KEPT + z]


def late_body(
    place, kept, cell, low, mid, high, above, below, zs, zs_left, zs_right, old_e, old_h,
    out_e, out_h, f,
):
    at_back = place[0] == place[1] - 1
    base = PLANES - KEPT

    @pl.when(at_back)
    def _():
        out_e[...] = old_e[...]
        out_h[...] = old_h[...]

    @pl.when(jnp.logical_not(at_back))
    def _():
        for c in range(FIELDS):
            for z in range(KEPT):
                f[c, z] = kept[c, z]
            packed = jnp.concatenate([zs_left[c // 2, 12:16], zs[c // 2], zs_right[c // 2, 0:4]], 0)
            for z in range(DEPTHS[c]):
                at = sent_index(c, z)
                dst = f.at[c, KEPT + z]
                dst[:, 0:LANES] = jnp.concatenate(
                    [above[at], low[at], mid[at], high[at], below[at]], 0
                )
                k = (c % 2) * 8 + z
                dst[:, LANES:WIDE] = pltpu.roll(packed, (2 * LANES - 8 * k - HALO) % LANES, 1)

        def step(s):
            loop(PLANES - s - base, PLANES + DEEP - s - base, lambda p: whole_plane(f, cell, p))

        loop(1, STEPS + 1, step)

        def give(z):
            for c in range(3):
                at = z + PLANES // 2 + STEPS - base
                out_e[c, z] = f[c, at, HALO : HALO + ROWS, 0:LANES]
                out_h[c, z] = f[3 + c, at, HALO : HALO + ROWS, 0:LANES]

        loop(0, PLANES // 2, give)


def shards(electric, magnetic, aux_state, material, kerr_strength):
    n_gz, n_gx, n_gy = (lax.axis_size(a) for a in ("gz", "gx", "gy"))
    position = lax.axis_index("gz")
    place = jnp.stack([position, jnp.int32(n_gz)]).astype(jnp.int32)
    end = (position != 0).astype(jnp.int32)
    rates = lax.dynamic_index_in_dim(decay_rates(PML), end, 0, keepdims=False)
    aux = lax.dynamic_slice_in_dim(aux_state, end, 1, 1)
    mat = material.astype(F32)

    back = [(i, i - 1) for i in range(1, n_gz)]
    to_right = [(i, (i + 1) % n_gx) for i in range(n_gx)]
    to_left = [(i, (i - 1) % n_gx) for i in range(n_gx)]
    swap = [(i, (i + 1) % n_gy) for i in range(n_gy)]
    back_swap = [(i * n_gy + j, (i - 1) * n_gy + k) for i in range(1, n_gz) for j, k in swap]

    low, mid, high, zs, ys = call(
        pack_body,
        [(SENT, 4, LANES), (SENT, 8, LANES), (SENT, 4, LANES), (3, ROWS, LANES), (GROUPS, ROWS, LANES)],
        [VMEM] * 4,
    )(electric, magnetic, aux, mat)
    ys = lax.ppermute(ys, "gy", swap)
    low = lax.ppermute(low, "gz", back)
    high = lax.ppermute(high, "gz", back)
    zs = lax.ppermute(zs, ("gz", "gy"), back_swap)
    mid = lax.ppermute(mid, "gz", back)

    rows = (TAKEN + GROUPS, 4, LANES)
    my_first, my_last = call(rows_body, [rows, rows], [VMEM] * 5)(electric, magnetic, aux, mat, ys)
    from_left = lax.ppermute(my_last, "gx", to_right)
    from_right = lax.ppermute(my_first, "gx", to_left)

    part = (3, PLANES, ROWS, LANES)
    out_e, out_h, kept, cell = call(
        early_body,
        [part, part, (FIELDS, KEPT, TALL, WIDE), (2, TALL, WIDE)],
        [SMEM] * 3 + [VMEM] * 7,
        [
            pltpu.VMEM((FIELDS, PLANES + STEPS, TALL, WIDE), F32),
            pltpu.VMEM((4, PML, TALL, WIDE), F32),
        ],
        cost_estimate=pl.CostEstimate(flops=20_000_000, bytes_accessed=6_000_000, transcendentals=0),
    )(place, rates, kerr_strength, electric, magnetic, aux, mat, ys, from_left, from_right)

    above = lax.ppermute(high, "gx", to_right)
    below = lax.ppermute(low, "gx", to_left)
    zs_left = lax.ppermute(zs, "gx", to_right)
    zs_right = lax.ppermute(zs, "gx", to_left)

    half = pl.BlockSpec((3, PLANES // 2, ROWS, LANES), lambda i: (0, 1, 0, 0))

    out_e, out_h = call(
        late_body,
        [part, part],
        [SMEM] + [VMEM] * 10 + [half, half],
        [pltpu.VMEM((FIELDS, KEPT + DEEP, TALL, WIDE), F32)],
        grid=(1,),
        out_specs=[half, half],
        input_output_aliases={11: 0, 12: 1},
    )(place, kept, cell, low, mid, high, above, below, zs, zs_left, zs_right, out_e, out_h)
    return (out_e, out_h)


def solution(mesh):
    in_specs = (
        P(None, "gz", "gx", "gy"),
        P(None, "gz", "gx", "gy"),
        P(None, None, None, "gx", "gy"),
        P("gx", "gy"),
        P(),
    )
    out_specs = (P(None, "gz", "gx", "gy"), P(None, "gz", "gx", "gy"))
    return jax.shard_map(shards, mesh=mesh, in_specs=in_specs, out_specs=out_specs, check_vma=False)
```

time: 168 us -> 46.9 us (0.28)
  local copies, waits for them, and re-layouts: 54 us -> 2.72 us
  starting transfers between devices: 60.9 us -> 23.2 us
  waiting for transfers between devices: 37 us -> 1.78 us
  Pallas kernels: 0 us -> 17.8 us
  other arithmetic: 11.8 us -> 0.1 us
    ppermute x28 -> x11, starting transfers between devices: 60.9 us -> 23.2 us  [the longest x1 8.83 us: shards(): zs = lax.ppermute(zs, ('gz', 'gy'), back_swap)]
    ppermute x28 -> x11, waiting for transfers between devices: 37 us -> 1.78 us  [the longest x1 1.76 us: shards(): from_left = lax.ppermute(my_last, 'gx', to_right)]
    unnamed x154 -> x12, local copies, waits for them, and re-layouts: 24 us -> 2.7 us
    pallas_call x0 -> x4, Pallas kernels: none -> 17.8 us  [the longest x1 9.83 us: shards(): call(early_body, [part, part, (FIELDS, KEPT, TALL, WIDE), (2, TALL, WIDE)...]
    concatenate x53 -> x0, local copies, waits for them, and re-layouts: 16.6 us -> none  [the longest x20 7.99 us: backward_y(): return values - jnp.concatenate([edge[:, :, None], values[:, :, :-1]], 2)]
    slice x57 -> x0, local copies, waits for them, and re-layouts: 8.51 us -> none  [the longest x8 2.68 us: backward_z(): return values - jnp.concatenate([edge, values[:-1]], 0)]
    unnamed x12 -> x0, other arithmetic: 6.64 us -> none
    squeeze x11 -> x1, local copies, waits for them, and re-layouts: 3.47 us -> 0.01 us  [shards(): rates = lax.dynamic_index_in_dim(decay_rates(PML), end, 0, keepdims=False)]
  transfers between devices with their start and end apart: 28 -> 11, of which waited for: 16 -> 1; matrix products, arithmetic and copies ran while one was open for 12% -> 0% of each run, Pallas kernels for 0% -> 21%
where the time goes in v1:
time: 46.9 us; the launch traced here: 46.4 us
  starting transfers between devices  23.2 us (49%)
  Pallas kernels  17.8 us (38%)
  local copies, waits for them, and re-layouts  2.72 us (6%)
  waiting for transfers between devices  1.78 us (4%)
  between operations  0.8 us (2%)
    pallas_call x1, Pallas kernels, shards(): call(early_body, [part, part, (FIELDS, KEPT, TALL, WIDE), (2, TALL, WIDE)...  9.83 us
    ppermute x1, starting transfers between devices, shards(): zs = lax.ppermute(zs, ('gz', 'gy'), back_swap)  8.83 us
    pallas_call x1, Pallas kernels, shards(): call(late_body, [part, part], [SMEM] + [VMEM] * 10 + [half, half], [pltpu...  7.52 us
    ppermute x1, starting transfers between devices, shards(): high = lax.ppermute(high, 'gz', back)  3.36 us
    ppermute x1, starting transfers between devices, shards(): below = lax.ppermute(low, 'gx', to_left)  2.95 us
    ppermute x1, starting transfers between devices, shards(): from_right = lax.ppermute(my_first, 'gx', to_left)  2.94 us
    unnamed x12, local copies, waits for them, and re-layouts  2.7 us
    ppermute x1, starting transfers between devices, shards(): low = lax.ppermute(low, 'gz', back)  2.46 us
  transfers between devices with their start and end apart: 11, of which 1 were waited for; matrix products, arithmetic and copies ran while one was open for 0% of the time, Pallas kernels for 21%

profile of v1, /device:TPU:56, one launch (start us, length us, event | category | flops | bytes accessed | tf_op | source)
XLA Modules:
  0.0 46.4 jit_solution(5479469938869224980)
XLA Ops:
  0.6 0.0 copy-start
  0.7 0.7 %copy-done.5 = s32[16,128]{1,0:T(8,128)S(1)} copy-done((s32[16,128]{1,0:T(8,128)S(1)}, s32[16,128]{1,0:T(8,128)}, u32[]{:S(2)}) %copy-start.5) | copy-done | bytes 8216
  1.4 0.3 copy-done
  1.7 0.1 copy-done.1
  1.8 1.0 %copy-done.2 = f32[3,16,16,128]{3,2,1,0:T(8,128)S(1)} copy-done((f32[3,16,16,128]{3,2,1,0:T(8,128)S(1)}, f32[3,16,16,128]{3,2,1,0:T(8,128)}, u32[]{:S(2)}) %copy-start.2) | copy-done | bytes 393240
  2.8 0.4 shard_map.68
  3.2 0.2 collective-permute-start
  3.4 8.8 %collective-permute-start.8 = (f32[3,16,128]{2,1,0:T(8,128)S(1)}, f32[3,16,128]{2,1,0:T(8,128)S(1)}, u32[]{:S(2)}, u32[]{:S(2)}) collective-permute-start(f32[3,16,128]{2,1,0:T(8,128)S(1)} %get-tuple-element.21), channel_id=1, source_target_pairs={{16,1},{17,0},{32,17},{33,16},{48,33},{49,32},{64,49},{65,48},{80,... | collective-permute-start | bytes 73736 | tf_op jit(solution)/shard_map/ppermute | solution.py:312
  12.2 3.4 %collective-permute-start.5 = (f32[44,4,128]{2,1,0:T(4,128)S(1)}, f32[44,4,128]{2,1,0:T(4,128)S(1)}, u32[]{:S(2)}, u32[]{:S(2)}) collective-permute-start(f32[44,4,128]{2,1,0:T(4,128)S(1)} %get-tuple-element.20), channel_id=1, source_target_pairs={{16,0},{32,16},{48,32},{64,48},{80,64},{96,80},{112,96},{128,112},... | collective-permute-start | bytes 270344 | tf_op jit(solution)/shard_map/ppermute | solution.py:311
  15.6 2.5 %collective-permute-start.3 = (f32[44,4,128]{2,1,0:T(4,128)S(1)}, f32[44,4,128]{2,1,0:T(4,128)S(1)}, u32[]{:S(2)}, u32[]{:S(2)}) collective-permute-start(f32[44,4,128]{2,1,0:T(4,128)S(1)} %get-tuple-element.18), channel_id=1, source_target_pairs={{16,0},{32,16},{48,32},{64,48},{80,64},{96,80},{112,96},{128,112},... | collective-permute-start | bytes 270344 | tf_op jit(solution)/shard_map/ppermute | solution.py:310
  18.1 0.0 collective-permute-done.ystrip
  18.1 0.1 shard_map.69
  18.2 0.0 collective-permute-start.1
  18.2 2.9 %collective-permute-start.2 = (f32[138,4,128]{2,1,0:T(4,128)S(1)}, f32[138,4,128]{2,1,0:T(4,128)S(1)}, u32[]{:S(2)}, u32[]{:S(2)}) collective-permute-start(f32[138,4,128]{2,1,0:T(4,128)S(1)} %get-tuple-element.15), channel_id=1, source_target_pairs={{0,14},{2,0},{4,2},{6,4},{8,6},{10,8},{12,10},{14,12},{1,15},{3,1}... | collective-permute-start | bytes 847880 | tf_op jit(solution)/shard_map/ppermute | solution.py:318
  21.2 0.0 collective-permute-done.8.zs
  21.2 1.9 %collective-permute-start.4 = (f32[44,8,128]{2,1,0:T(8,128)S(1)}, f32[44,8,128]{2,1,0:T(8,128)S(1)}, u32[]{:S(2)}, u32[]{:S(2)}) collective-permute-start(f32[44,8,128]{2,1,0:T(8,128)S(1)} %get-tuple-element.19), channel_id=1, source_target_pairs={{16,0},{32,16},{48,32},{64,48},{80,64},{96,80},{112,96},{128,112},... | collective-permute-start | bytes 540680 | tf_op jit(solution)/shard_map/ppermute | solution.py:313
  23.1 0.0 collective-permute-done.5.high
  23.1 0.0 collective-permute-start.10
  23.2 0.0 collective-permute-done.3.low
  23.2 0.5 %collective-permute-start.9 = (f32[3,16,128]{2,1,0:T(8,128)S(1)}, f32[3,16,128]{2,1,0:T(8,128)S(1)}, u32[]{:S(2)}, u32[]{:S(2)}) collective-permute-start(f32[3,16,128]{2,1,0:T(8,128)S(1)} %collective-permute-done.8.zs), channel_id=1, source_target_pairs={{0,2},{2,4},{4,6},{6,8},{8,10},{10,12},{12,14},{14,0},{1,3},{3,5},... | collective-permute-start | bytes 73736 | tf_op jit(solution)/shard_map/ppermute | solution.py:334
  23.7 1.8 %collective-permute-done.1.left = f32[138,4,128]{2,1,0:T(4,128)S(1)} collective-permute-done((f32[138,4,128]{2,1,0:T(4,128)S(1)}, f32[138,4,128]{2,1,0:T(4,128)S(1)}, u32[]{:S(2)}, u32[]{:S(2)}) %collective-permute-start.1) | collective-permute-done | bytes 282656 | tf_op jit(solution)/shard_map/ppermute | solution.py:317
  25.4 0.0 collective-permute-start.6
  25.4 0.0 collective-permute-done.2.right
  25.4 3.0 %collective-permute-start.7 = (f32[44,4,128]{2,1,0:T(4,128)S(1)}, f32[44,4,128]{2,1,0:T(4,128)S(1)}, u32[]{:S(2)}, u32[]{:S(2)}) collective-permute-start(f32[44,4,128]{2,1,0:T(4,128)S(1)} %collective-permute-done.3.low), channel_id=1, source_target_pairs={{0,14},{2,0},{4,2},{6,4},{8,6},{10,8},{12,10},{14,12},{1,15},{3,1}... | collective-permute-start | bytes 270344 | tf_op jit(solution)/shard_map/ppermute | solution.py:333
  28.4 0.1 pad_add_fusion.place
  28.5 0.6 %copy-done.4 = f32[2]{0:T(128)S(1)} copy-done((f32[2]{0:T(128)S(1)}, f32[2]{0:T(128)}, u32[]{:S(2)}) %copy-start.4) | copy-done | bytes 32
  29.0 9.8 %shard_map.70 = (f32[3,16,16,128]{3,2,1,0:T(8,128)}, f32[3,16,16,128]{3,2,1,0:T(8,128)}, f32[6,5,24,256]{3,2,1,0:T(8,128)S(1)}, f32[2,24,256]{2,1,0:T(8,128)S(1)}) custom-call(s32[2]{0:T(128)S(1)} %pad_add_fusion.place, f32[8]{0:T(128)S(1)} %dynamic-slice_bitcast_fusion.rates, f32[2]{0:T(128)S(1)} %copy-done.4, f32[3,16,16,128]{3,2,1,0:T(8,128)S(1)} %copy-done.1, ...), custom_call_target="tpu_custom_call" | custom-call | flops 20000000 | bytes 6000000 | tf_op jit(solution)/shard_map/pallas_call | solution.py:321
  38.9 0.0 collective-permute-done.10.zs_right
  38.9 0.0 collective-permute-done.9.zs_left
  38.9 0.0 collective-permute-done.6.above
  38.9 0.0 collective-permute-done.7.below
  38.9 7.5 %shard_map.71 = (f32[3,16,16,128]{3,2,1,0:T(8,128)}, f32[3,16,16,128]{3,2,1,0:T(8,128)}) custom-call(s32[2]{0:T(128)S(1)} %pad_add_fusion.place, f32[6,5,24,256]{3,2,1,0:T(8,128)S(1)} %get-tuple-element.16.kept, f32[2,24,256]{2,1,0:T(8,128)S(1)} %get-tuple-element.17.cell, ...), custom_call_target="tpu_custom_call", output_to_operand_aliasing={{0}: (11, {}), {1}: (12, {})} | custom-call | tf_op jit(solution)/shard_map/pallas_call | solution.py:339
  (12 shorter events, 0.1 us)
Async XLA Ops:
  0.6 1.1 %copy-start = (f32[4,2,8,16,128]{4,3,2,1,0:T(8,128)S(1)}, f32[4,2,8,16,128]{4,3,2,1,0:T(8,128)}, u32[]{:S(2)}) copy-start(f32[4,2,8,16,128]{4,3,2,1,0:T(8,128)} %param.7) | copy-start | bytes 1572868
  0.6 0.8 %copy-start.5 = (s32[16,128]{1,0:T(8,128)S(1)}, s32[16,128]{1,0:T(8,128)}, u32[]{:S(2)}) copy-start(s32[16,128]{1,0:T(8,128)} %param.8) | copy-start | bytes 24580
  0.7 1.1 %copy-start.1 = (f32[3,16,16,128]{3,2,1,0:T(8,128)S(1)}, f32[3,16,16,128]{3,2,1,0:T(8,128)}, u32[]{:S(2)}) copy-start(f32[3,16,16,128]{3,2,1,0:T(8,128)} %e.5) | copy-start | bytes 1179652
  1.8 1.0 %copy-start.2 = (f32[3,16,16,128]{3,2,1,0:T(8,128)S(1)}, f32[3,16,16,128]{3,2,1,0:T(8,128)}, u32[]{:S(2)}) copy-start(f32[3,16,16,128]{3,2,1,0:T(8,128)} %h.5) | copy-start | bytes 1179652
  2.8 15.3 %copy-start.3 = (f32[3,16,16,128]{3,2,1,0:T(8,128)S(1)}, f32[3,16,16,128]{3,2,1,0:T(8,128)}, u32[]{:S(2)}) copy-start(f32[3,16,16,128]{3,2,1,0:T(8,128)} %h.5) | copy-start | bytes 1179652
  3.2 14.9 %collective-permute-start = (f32[9,16,128]{2,1,0:T(8,128)S(1)}, f32[9,16,128]{2,1,0:T(8,128)S(1)}, u32[]{:S(2)}, u32[]{:S(2)}) collective-permute-start(f32[9,16,128]{2,1,0:T(8,128)S(1)} %get-tuple-element.13), channel_id=1, source_target_pairs={{0,1},{1,0},{2,3},{3,2},{4,5},{5,4},{6,7},{7,6},{8,9},{9,8},{10,11... | collective-permute-start | bytes 221192 | tf_op jit(solution)/shard_map/ppermute | solution.py:309
  3.4 17.8 %collective-permute-start.8 = (f32[3,16,128]{2,1,0:T(8,128)S(1)}, f32[3,16,128]{2,1,0:T(8,128)S(1)}, u32[]{:S(2)}, u32[]{:S(2)}) collective-permute-start(f32[3,16,128]{2,1,0:T(8,128)S(1)} %get-tuple-element.21), channel_id=1, source_target_pairs={{16,1},{17,0},{32,17},{33,16},{48,33},{49,32},{64,49},{65,48},{80,... | collective-permute-start | bytes 73736 | tf_op jit(solution)/shard_map/ppermute | solution.py:312
  12.2 10.9 %collective-permute-start.5 = (f32[44,4,128]{2,1,0:T(4,128)S(1)}, f32[44,4,128]{2,1,0:T(4,128)S(1)}, u32[]{:S(2)}, u32[]{:S(2)}) collective-permute-start(f32[44,4,128]{2,1,0:T(4,128)S(1)} %get-tuple-element.20), channel_id=1, source_target_pairs={{16,0},{32,16},{48,32},{64,48},{80,64},{96,80},{112,96},{128,112},... | collective-permute-start | bytes 270344 | tf_op jit(solution)/shard_map/ppermute | solution.py:311
  15.6 7.6 %collective-permute-start.3 = (f32[44,4,128]{2,1,0:T(4,128)S(1)}, f32[44,4,128]{2,1,0:T(4,128)S(1)}, u32[]{:S(2)}, u32[]{:S(2)}) collective-permute-start(f32[44,4,128]{2,1,0:T(4,128)S(1)} %get-tuple-element.18), channel_id=1, source_target_pairs={{16,0},{32,16},{48,32},{64,48},{80,64},{96,80},{112,96},{128,112},... | collective-permute-start | bytes 270344 | tf_op jit(solution)/shard_map/ppermute | solution.py:310
  18.2 7.2 %collective-permute-start.1 = (f32[138,4,128]{2,1,0:T(4,128)S(1)}, f32[138,4,128]{2,1,0:T(4,128)S(1)}, u32[]{:S(2)}, u32[]{:S(2)}) collective-permute-start(f32[138,4,128]{2,1,0:T(4,128)S(1)} %get-tuple-element.14), channel_id=1, source_target_pairs={{0,2},{2,4},{4,6},{6,8},{8,10},{10,12},{12,14},{14,0},{1,3},{3,5},... | collective-permute-start | bytes 847880 | tf_op jit(solution)/shard_map/ppermute | solution.py:317
  18.2 7.2 %collective-permute-start.2 = (f32[138,4,128]{2,1,0:T(4,128)S(1)}, f32[138,4,128]{2,1,0:T(4,128)S(1)}, u32[]{:S(2)}, u32[]{:S(2)}) collective-permute-start(f32[138,4,128]{2,1,0:T(4,128)S(1)} %get-tuple-element.15), channel_id=1, source_target_pairs={{0,14},{2,0},{4,2},{6,4},{8,6},{10,8},{12,10},{14,12},{1,15},{3,1}... | collective-permute-start | bytes 847880 | tf_op jit(solution)/shard_map/ppermute | solution.py:318
  21.2 17.7 %collective-permute-start.4 = (f32[44,8,128]{2,1,0:T(8,128)S(1)}, f32[44,8,128]{2,1,0:T(8,128)S(1)}, u32[]{:S(2)}, u32[]{:S(2)}) collective-permute-start(f32[44,8,128]{2,1,0:T(8,128)S(1)} %get-tuple-element.19), channel_id=1, source_target_pairs={{16,0},{32,16},{48,32},{64,48},{80,64},{96,80},{112,96},{128,112},... | collective-permute-start | bytes 540680 | tf_op jit(solution)/shard_map/ppermute | solution.py:313
  23.1 15.7 %collective-permute-start.10 = (f32[3,16,128]{2,1,0:T(8,128)S(1)}, f32[3,16,128]{2,1,0:T(8,128)S(1)}, u32[]{:S(2)}, u32[]{:S(2)}) collective-permute-start(f32[3,16,128]{2,1,0:T(8,128)S(1)} %collective-permute-done.8.zs), channel_id=1, source_target_pairs={{0,14},{2,0},{4,2},{6,4},{8,6},{10,8},{12,10},{14,12},{1,15},{3,1}... | collective-permute-start | bytes 73736 | tf_op jit(solution)/shard_map/ppermute | solution.py:335
  23.2 15.7 %collective-permute-start.9 = (f32[3,16,128]{2,1,0:T(8,128)S(1)}, f32[3,16,128]{2,1,0:T(8,128)S(1)}, u32[]{:S(2)}, u32[]{:S(2)}) collective-permute-start(f32[3,16,128]{2,1,0:T(8,128)S(1)} %collective-permute-done.8.zs), channel_id=1, source_target_pairs={{0,2},{2,4},{4,6},{6,8},{8,10},{10,12},{12,14},{14,0},{1,3},{3,5},... | collective-permute-start | bytes 73736 | tf_op jit(solution)/shard_map/ppermute | solution.py:334
  25.4 13.5 %collective-permute-start.6 = (f32[44,4,128]{2,1,0:T(4,128)S(1)}, f32[44,4,128]{2,1,0:T(4,128)S(1)}, u32[]{:S(2)}, u32[]{:S(2)}) collective-permute-start(f32[44,4,128]{2,1,0:T(4,128)S(1)} %collective-permute-done.5.high), channel_id=1, source_target_pairs={{0,2},{2,4},{4,6},{6,8},{8,10},{10,12},{12,14},{14,0},{1,3},{3,5},... | collective-permute-start | bytes 270344 | tf_op jit(solution)/shard_map/ppermute | solution.py:332
  25.4 13.5 %collective-permute-start.7 = (f32[44,4,128]{2,1,0:T(4,128)S(1)}, f32[44,4,128]{2,1,0:T(4,128)S(1)}, u32[]{:S(2)}, u32[]{:S(2)}) collective-permute-start(f32[44,4,128]{2,1,0:T(4,128)S(1)} %collective-permute-done.3.low), channel_id=1, source_target_pairs={{0,14},{2,0},{4,2},{6,4},{8,6},{10,8},{12,10},{14,12},{1,15},{3,1}... | collective-permute-start | bytes 270344 | tf_op jit(solution)/shard_map/ppermute | solution.py:333
  28.4 0.7 %copy-start.4 = (f32[2]{0:T(128)S(1)}, f32[2]{0:T(128)}, u32[]{:S(2)}) copy-start(f32[2]{0:T(128)} %kerr.1) | copy-start | bytes 28

commit v2 on v1

v2 whole, which is shorter than its diff:
```python
import math

import jax
import jax.numpy as jnp
from jax import lax
from jax.experimental import pallas as pl
from jax.experimental.pallas import tpu as pltpu
from jax.sharding import PartitionSpec as P

PML = 8
STEPS = 4
HALO = 4
DEEP = 8
PLANES = 16
ROWS = 16
LANES = 128
TALL = ROWS + 2 * HALO
WIDE = 2 * LANES
FIELDS = 6
DEPTHS = (8, 8, 7, 7, 7, 7)
SENT = sum(DEPTHS)
OWN = FIELDS * PLANES
AUX = 4 * PML
MAT = OWN + AUX
TAKEN = MAT + 1
GROUPS = (TAKEN + 15) // 16
KEPT = 5

courant = 0.5
pml_rate = 3.0
eps_clad = 2.085
eps_core = 4.0

VMEM = pl.BlockSpec(memory_space=pltpu.VMEM)
HBM = pl.BlockSpec(memory_space=pltpu.HBM)
F32 = jnp.float32


def front_rate(k):
    return math.exp(-pml_rate * ((PML - k) / PML) ** 3)


def back_rate(k):
    return math.exp(-pml_rate * ((k + 1) / PML) ** 3)


def ends():
    at = lax.axis_index("gz")
    return at == 0, at == lax.axis_size("gz") - 1


def sent_index(c, z):
    return sum(DEPTHS[:c]) + z


def call(body, out_shape, in_specs, scratch=(), **more):
    n_out = len(out_shape)
    more.setdefault("out_specs", [VMEM] * n_out)
    return pl.pallas_call(
        body,
        out_shape=[jax.ShapeDtypeStruct(s, F32) for s in out_shape],
        in_specs=in_specs,
        scratch_shapes=list(scratch),
        compiler_params=pltpu.CompilerParams(vmem_limit_bytes=40 * 1024 * 1024),
        cost_estimate=COST.get(body),
        **more,
    )


def strip(tiles):
    lane = lax.broadcasted_iota(jnp.int32, (ROWS, LANES), 1) // 8
    out = jnp.zeros((ROWS, LANES), F32)
    for k, tile in enumerate(tiles):
        out = jnp.where(lane == k, pltpu.roll(tile, (8 * k + HALO) % LANES, 1), out)
    return out


def unstrip(packed, k):
    return pltpu.roll(packed, (2 * LANES - 8 * k - HALO) % LANES, 1)


def deep_body(e, h, edge, mid, zstrip, token):
    for c in range(FIELDS):
        src = e if c < 3 else h
        for z in range(DEPTHS[c]):
            plane = src[c % 3, z]
            at = sent_index(c, z)
            edge[at] = plane[0:4]
            edge[SENT + at] = plane[12:16]
            mid[at] = plane[4:12]
        if c % 2:
            pair = [(c - 1, z) for z in range(DEEP)] + [(c, z) for z in range(DEEP)]
            zstrip[c // 2] = strip([(e if i < 3 else h)[i % 3, z] for i, z in pair])
    token[...] = jnp.zeros((8, LANES), F32)


def strip_body(e, h, aux, material, kerr, token, ystrip, chosen, mat, kerrs, sem):
    at_front, _ = ends()
    copy = pltpu.make_async_copy(aux.at[:, pl.ds(jnp.where(at_front, 0, 1), 1)], chosen, sem)
    copy.start()
    for c in range(FIELDS):
        src = e if c < 3 else h
        ystrip[c] = strip([src[c % 3, z] for z in range(PLANES)])
    mat[...] = material[...].astype(F32)
    ystrip[FIELDS + 2] = strip([mat[...]])
    for i in range(2):
        kerrs[i] = jnp.broadcast_to(kerr[0:1, i : i + 1], (8, LANES))
    copy.wait()
    for j in range(2):
        ystrip[FIELDS + j] = strip([chosen[2 * j + k // PML, 0, k % PML] for k in range(16)])


def tall(own, above, below):
    return jnp.concatenate([above, own, below], 0)


def relay_body(edge, zstrip, to_left, to_right):
    for at in range(SENT):
        to_left[at] = edge[at]
        to_right[at] = edge[SENT + at]
    for j in range(3):
        to_left[SENT + j] = zstrip[j, 0:4]
        to_right[SENT + j] = zstrip[j, 12:16]


def gather_body(edge, left, right, zstrip, cell, planes, strips):
    for at in range(SENT):
        planes[at, 0] = jnp.concatenate([left[at], edge[at]], 0)
        planes[at, 1] = jnp.concatenate([edge[SENT + at], right[at]], 0)
    for j in range(3):
        strips[j] = tall(zstrip[j], left[SENT + j], right[SENT + j])


def rows_body(e, h, aux, mat, ystrip, to_left, to_right):
    def put(at, tile):
        to_left[at] = tile[0:4]
        to_right[at] = tile[12:16]

    for c in range(FIELDS):
        src = e if c < 3 else h
        for z in range(PLANES):
            put(c * PLANES + z, src[c % 3, z])
    for a in range(4):
        for k in range(PML):
            put(OWN + a * PML + k, aux[a, 0, k])
    put(MAT, mat[...])
    for g in range(GROUPS):
        put(TAKEN + g, ystrip[g])


def forward(value, axis):
    return pltpu.roll(value, value.shape[axis] - 1, axis) - value


def backward(value, axis):
    return value - pltpu.roll(value, 1, axis)


def absorb(slope, state, index, k, rate):
    old = state[index, k]
    kept = rate * (slope + old)
    state[index, k] = kept - slope
    return kept


def magnetic_plane(read, write, p, layer=None):
    ex, ey, ez = (read(c, p) for c in range(3))
    slope_y = read(1, p + 1) - ey
    slope_x = read(0, p + 1) - ex
    if layer is not None:
        state, k, rate = layer
        slope_y = absorb(slope_y, state, 0, k, rate)
        slope_x = absorb(slope_x, state, 1, k, rate)
    write(3, p, read(3, p) - courant * (forward(ez, 1) - slope_y))
    write(4, p, read(4, p) - courant * (slope_x - forward(ez, 0)))
    write(5, p, read(5, p) - courant * (forward(ey, 0) - forward(ex, 1)))


def electric_plane(read, write, cell, p, layer=None):
    ex, ey, ez, hx, hy, hz = (read(c, p) for c in range(FIELDS))
    factor = courant / (cell[0] + cell[1] * (ex * ex + ey * ey + ez * ez))
    slope_hy = hy - read(4, p - 1)
    slope_hx = hx - read(3, p - 1)
    if layer is not None:
        state, k, rate = layer
        slope_hy = absorb(slope_hy, state, 2, k, rate)
        slope_hx = absorb(slope_hx, state, 3, k, rate)
    write(0, p, ex + factor * (backward(hz, 1) - slope_hy))
    write(1, p, ey + factor * (slope_hx - backward(hz, 0)))
    write(2, p, ez + factor * (backward(hy, 0) - backward(hx, 1)))


def inner(value):
    return value[HALO : HALO + ROWS, 0:LANES]


def early_body(
    kerr, e, h, aux, mat, ystrip, left, right,
    out_e, out_h, kept, cell, f, state, done, sems,
):
    at_front, at_back = ends()

    def stripe(g):
        return tall(ystrip[g], left[TAKEN + g], right[TAKEN + g])

    def fill(dst, own, at):
        dst[:, 0:LANES] = tall(own, left[at], right[at])

    for c in range(FIELDS):
        src = e if c < 3 else h
        packed = stripe(c)
        for z in range(PLANES):
            dst = f.at[c, z]
            fill(dst, src[c % 3, z], c * PLANES + z)
            dst[:, LANES:WIDE] = unstrip(packed, z)

    flag_own = tall(mat[...], left[MAT], right[MAT])
    flag = jnp.concatenate([flag_own, unstrip(stripe(FIELDS + 2), 0)], 1) == 1.0
    cell[0] = jnp.where(flag, eps_core, eps_clad)
    cell[1] = jnp.where(flag, kerr[1, 0:1, 0:1], kerr[0, 0:1, 0:1])

    @pl.when(at_front | at_back)
    def _():
        for j in range(2):
            packed = stripe(FIELDS + j)
            for k in range(16):
                a, z = 2 * j + k // PML, k % PML
                dst = state.at[a, z]
                fill(dst, aux[a, 0, z], OWN + a * PML + z)
                dst[:, LANES:WIDE] = unstrip(packed, k)

    @pl.when(at_back)
    def _():
        for c in range(FIELDS):
            for z in range(STEPS):
                f[c, PLANES + z] = jnp.zeros((TALL, WIDE), F32)

    def read(c, p):
        return f[c, p]

    def write(c, p, value):
        f[c, p] = value

    def run(last, layer_from, rate):
        for s in range(1, STEPS + 1):

            def layer(p):
                k = -1 if layer_from is None else p - layer_from(s)
                return (state, k, rate(k)) if 0 <= k < PML else None

            for p in range(s - 1, last(s) + 1):
                magnetic_plane(read, write, p, layer(p))
            for p in range(s, last(s) + 1):
                electric_plane(read, write, cell, p, layer(p))

    @pl.when(at_front)
    def _():
        run(lambda s: PLANES - 1 - s, lambda s: s - 1, front_rate)

    @pl.when(at_back)
    def _():
        run(lambda s: PLANES - 2 + s, lambda s: PLANES - PML + s - 1, back_rate)

    @pl.when(jnp.logical_not(at_front | at_back))
    def _():
        run(lambda s: PLANES - 1 - s, None, None)

    def send(at):
        span = pl.ds(at * PLANES // 2, PLANES // 2)
        for z in range(at * PLANES // 2, (at + 1) * PLANES // 2):
            for c in range(FIELDS):
                done[c, z] = inner(f[c, z + STEPS])
        copies = [
            pltpu.make_async_copy(done.at[pl.ds(3 * i, 3), span], out.at[:, span], sems.at[2 * at + i])
            for i, out in enumerate((out_e, out_h))
        ]
        for copy in copies:
            copy.start()
        return copies

    first = send(0)

    @pl.when(at_back)
    def _():
        for copy in send(1):
            copy.wait()

    for c in range(FIELDS):
        for z in range(KEPT):
            kept[c, z] = f[c, PLANES - KEPT + z]
    for copy in first:
        copy.wait()


def late_body(kept, cell, planes, strips, mid, old_e, old_h, out_e, out_h, f, done, sems):
    base = PLANES - KEPT
    span = pl.ds(PLANES // 2, PLANES // 2)

    @pl.when(jnp.logical_not(ends()[1]))
    def _():
        made = set()

        def read(c, p):
            if (c, p) in made:
                return f[c, p - base]
            if p < PLANES:
                return kept[c, p - base]
            at = sent_index(c, p - PLANES)
            own = jnp.concatenate([planes[at, 0], mid[at], planes[at, 1]], 0)
            side = unstrip(strips[c // 2], (c % 2) * DEEP + p - PLANES)
            return jnp.concatenate([own, side], 1)

        def write(c, p, value):
            if s == STEPS:
                done[c, p - PLANES // 2 - STEPS] = inner(value)
                if c >= 3:
                    f[c, p - base] = value
            else:
                f[c, p - base] = value
            made.add((c, p))

        def send(i):
            return pltpu.make_async_copy(
                done.at[pl.ds(3 * i, 3)], (out_e, out_h)[i].at[:, span], sems.at[i]
            )

        for s in range(1, STEPS + 1):
            window = range(PLANES - s, PLANES + DEEP - s)
            for p in window:
                magnetic_plane(read, write, p)
            if s == STEPS:
                send(1).start()
            for p in window:
                electric_plane(read, write, cell, p)
        send(0).start()
        send(1).wait()
        send(0).wait()


COST = {relay_body: pl.CostEstimate(flops=3_000_000_000, bytes_accessed=3_000_000_000, transcendentals=0)}


def shards(electric, magnetic, aux_state, material, kerr_strength):
    n_gz, n_gx, n_gy = (lax.axis_size(a) for a in ("gz", "gx", "gy"))
    back = [(i, i - 1) for i in range(1, n_gz)]
    to_right = [(i, (i + 1) % n_gx) for i in range(n_gx)]
    to_left = [(i, (i - 1) % n_gx) for i in range(n_gx)]
    swap = [(i, (i + 1) % n_gy) for i in range(n_gy)]
    back_swap = [(i * n_gy + j, (i - 1) * n_gy + k) for i in range(1, n_gz) for j, k in swap]
    dma = pltpu.SemaphoreType.DMA

    edge, mid, zs, token = call(
        deep_body,
        [(2 * SENT, 4, LANES), (SENT, 8, LANES), (3, ROWS, LANES), (8, LANES)],
        [VMEM, VMEM],
    )(electric[:, :DEEP], magnetic[:, :DEEP])
    edge = lax.ppermute(edge, "gz", back)
    zs = lax.ppermute(zs, ("gz", "gy"), back_swap)
    mid = lax.ppermute(mid, "gz", back)

    ys, aux, mat, kerr = call(
        strip_body,
        [(GROUPS, ROWS, LANES), (4, 1, PML, ROWS, LANES), (ROWS, LANES), (2, 8, LANES)],
        [VMEM, VMEM, HBM, VMEM, VMEM, VMEM],
        [dma(())],
    )(electric, magnetic, aux_state, material, kerr_strength[None], token)
    ys = lax.ppermute(ys, "gy", swap)

    rows = (TAKEN + GROUPS, 4, LANES)
    my_first, my_last = call(rows_body, [rows, rows], [VMEM] * 5)(electric, magnetic, aux, mat, ys)
    from_left = lax.ppermute(my_last, "gx", to_right)
    from_right = lax.ppermute(my_first, "gx", to_left)

    relayed = (SENT + 3, 4, LANES)
    go_left, go_right = call(
        relay_body, [relayed, relayed], [VMEM] * 2
    )(edge, zs)
    left = lax.ppermute(go_right, "gx", to_right)
    right = lax.ppermute(go_left, "gx", to_left)

    part = (3, PLANES, ROWS, LANES)
    out_e, out_h, kept, cell = call(
        early_body,
        [part, part, (FIELDS, KEPT, TALL, WIDE), (2, TALL, WIDE)],
        [VMEM] * 8,
        [
            pltpu.VMEM((FIELDS, PLANES + STEPS, TALL, WIDE), F32),
            pltpu.VMEM((4, PML, TALL, WIDE), F32),
            pltpu.VMEM((FIELDS, PLANES, ROWS, LANES), F32),
            dma((4,)),
        ],
        out_specs=[HBM, HBM, VMEM, VMEM],
    )(kerr, electric, magnetic, aux, mat, ys, from_left, from_right)

    planes, strips = call(
        gather_body, [(SENT, 2, 8, LANES), (3, TALL, LANES)], [VMEM] * 5
    )(edge, left, right, zs, cell)

    out_e, out_h = call(
        late_body,
        [part, part],
        [VMEM] * 5 + [HBM, HBM],
        [
            pltpu.VMEM((FIELDS, KEPT + DEEP, TALL, WIDE), F32),
            pltpu.VMEM((FIELDS, PLANES // 2, ROWS, LANES), F32),
            dma((2,)),
        ],
        out_specs=[HBM, HBM],
        input_output_aliases={5: 0, 6: 1},
    )(kept, cell, planes, strips, mid, out_e, out_h)
    return (out_e, out_h)


def solution(mesh):
    in_specs = (
        P(None, "gz", "gx", "gy"),
        P(None, "gz", "gx", "gy"),
        P(None, None, None, "gx", "gy"),
        P("gx", "gy"),
        P(),
    )
    out_specs = (P(None, "gz", "gx", "gy"), P(None, "gz", "gx", "gy"))
    return jax.shard_map(shards, mesh=mesh, in_specs=in_specs, out_specs=out_specs, check_vma=False)
```

time: 46.9 us -> 34.4 us (0.73)
  the two profiles are of different devices: /device:TPU:56 before, /device:TPU:25 now
where the time goes in v2:
time: 34.4 us; the launch traced here: 34.2 us
  starting transfers between devices  18.1 us (53%)
  Pallas kernels  6.56 us (19%)
  waiting for transfers between devices  5.99 us (17%)
  local copies, waits for them, and re-layouts  2.78 us (8%)
  between operations  0.77 us (2%)
    ppermute x1, starting transfers between devices, shards(): edge = lax.ppermute(edge, 'gz', back)  8.11 us
    pallas_call x1, Pallas kernels, shards(): call(early_body, [part, part, (FIELDS, KEPT, TALL, WIDE), (2, TALL, WIDE)...  3.4 us
    ppermute x1, waiting for transfers between devices, shards(): from_right = lax.ppermute(my_first, 'gx', to_left)  2.77 us
    ppermute x1, starting transfers between devices, shards(): zs = lax.ppermute(zs, ('gz', 'gy'), back_swap)  2.61 us
    pallas_call x1, Pallas kernels, shards(): call(late_body, [part, part], [VMEM] * 5 + [HBM, HBM], [pltpu.VMEM((FIELD...  2.4 us
    ppermute x1, starting transfers between devices, shards(): mid = lax.ppermute(mid, 'gz', back)  2.38 us
    ppermute x1, starting transfers between devices, shards(): from_left = lax.ppermute(my_last, 'gx', to_right)  2.28 us
    unnamed x10, local copies, waits for them, and re-layouts  1.77 us
  transfers between devices with their start and end apart: 8, of which 3 were waited for; matrix products, arithmetic and copies ran while one was open for 0% of the time, Pallas kernels for 12%

profile of v2, /device:TPU:25, one launch (start us, length us, event | category | flops | bytes accessed | tf_op | source)
XLA Modules:
  0.0 34.2 jit_solution(12952368069506287317)
XLA Ops:
  0.6 0.0 copy-start.1
  0.6 1.0 %slice.6.e = f32[3,8,16,128]{3,2,1,0:T(8,128)S(1)} slice(f32[3,16,16,128]{3,2,1,0:T(8,128)} %e.5), slice={[0:3], [0:8], [0:16], [0:128]} | slice | bytes 393216 | tf_op jit(solution)/shard_map/slice | solution.py:356
  1.6 0.1 copy-done.1
  1.7 0.0 copy-start
  1.7 0.0 copy-start.3
  1.8 0.2 shard_map.68
  1.9 8.1 %collective-permute-start.3 = (f32[88,4,128]{2,1,0:T(4,128)S(1)}, f32[88,4,128]{2,1,0:T(4,128)S(1)}, u32[]{:S(2)}, u32[]{:S(2)}) collective-permute-start(f32[88,4,128]{2,1,0:T(4,128)S(1)} %get-tuple-element.29), channel_id=1, source_target_pairs={{16,0},{32,16},{48,32},{64,48},{80,64},{96,80},{112,96},{128,112},... | collective-permute-start | bytes 540680 | tf_op jit(solution)/shard_map/ppermute | solution.py:357
  10.0 0.0 copy-start.4
  10.1 0.0 copy-done
  10.1 0.0 copy-done.3
  10.1 0.6 %copy-done.4 = f32[2]{0:T(128)S(1)} copy-done((f32[2]{0:T(128)S(1)}, f32[2]{0:T(128)}, u32[]{:S(2)}) %copy-start.4) | copy-done | bytes 32
  10.7 1.0 %copy-done.2 = f32[4,2,8,16,128]{4,3,2,1,0:T(8,128)S(1)} copy-done((f32[4,2,8,16,128]{4,3,2,1,0:T(8,128)S(1)}, f32[4,2,8,16,128]{4,3,2,1,0:T(8,128)}, u32[]{:S(2)}) %copy-start.2) | copy-done | bytes 524312
  11.7 0.4 %shard_map.69 = (f32[9,16,128]{2,1,0:T(8,128)S(1)}, f32[4,1,8,16,128]{4,3,2,1,0:T(8,128)S(1)}, f32[16,128]{1,0:T(8,128)S(1)}, f32[2,8,128]{2,1,0:T(8,128)S(1)}) custom-call(f32[3,16,16,128]{3,2,1,0:T(8,128)S(1)} %copy-done, f32[3,16,16,128]{3,2,1,0:T(8,128)S(1)} %copy-done.1, f32[4,2,8,16,128]{4,3,2,1,0:T(8,128)S(1)} %copy-done.2, s32[16,128]{1,0:T(8,128)S(1)} %copy-done.3, ...), custom_call_target="tpu_custom_call" | custom-call | tf_op jit(solution)/shard_map/pallas_call | solution.py:361
  12.2 0.8 %collective-permute-start = (f32[9,16,128]{2,1,0:T(8,128)S(1)}, f32[9,16,128]{2,1,0:T(8,128)S(1)}, u32[]{:S(2)}, u32[]{:S(2)}) collective-permute-start(f32[9,16,128]{2,1,0:T(8,128)S(1)} %get-tuple-element.24), channel_id=1, source_target_pairs={{0,1},{1,0},{2,3},{3,2},{4,5},{5,4},{6,7},{7,6},{8,9},{9,8},{10,11... | collective-permute-start | bytes 221192 | tf_op jit(solution)/shard_map/ppermute | solution.py:367
  13.0 2.6 %collective-permute-start.4 = (f32[3,16,128]{2,1,0:T(8,128)S(1)}, f32[3,16,128]{2,1,0:T(8,128)S(1)}, u32[]{:S(2)}, u32[]{:S(2)}) collective-permute-start(f32[3,16,128]{2,1,0:T(8,128)S(1)} %get-tuple-element.30), channel_id=1, source_target_pairs={{16,1},{17,0},{32,17},{33,16},{48,33},{49,32},{64,49},{65,48},{80,... | collective-permute-start | bytes 73736 | tf_op jit(solution)/shard_map/ppermute | solution.py:358
  15.6 2.4 %collective-permute-start.7 = (f32[44,8,128]{2,1,0:T(8,128)S(1)}, f32[44,8,128]{2,1,0:T(8,128)S(1)}, u32[]{:S(2)}, u32[]{:S(2)}) collective-permute-start(f32[44,8,128]{2,1,0:T(8,128)S(1)} %get-tuple-element.35), channel_id=1, source_target_pairs={{16,0},{32,16},{48,32},{64,48},{80,64},{96,80},{112,96},{128,112},... | collective-permute-start | bytes 540680 | tf_op jit(solution)/shard_map/ppermute | solution.py:359
  18.0 1.6 %collective-permute-done.ystrip = f32[9,16,128]{2,1,0:T(8,128)S(1)} collective-permute-done((f32[9,16,128]{2,1,0:T(8,128)S(1)}, f32[9,16,128]{2,1,0:T(8,128)S(1)}, u32[]{:S(2)}, u32[]{:S(2)}) %collective-permute-start) | collective-permute-done | bytes 73760 | tf_op jit(solution)/shard_map/ppermute | solution.py:367
  19.6 0.1 shard_map.70
  19.7 2.3 %collective-permute-start.1 = (f32[138,4,128]{2,1,0:T(4,128)S(1)}, f32[138,4,128]{2,1,0:T(4,128)S(1)}, u32[]{:S(2)}, u32[]{:S(2)}) collective-permute-start(f32[138,4,128]{2,1,0:T(4,128)S(1)} %get-tuple-element.25), channel_id=1, source_target_pairs={{0,2},{2,4},{4,6},{6,8},{8,10},{10,12},{12,14},{14,0},{1,3},{3,5},... | collective-permute-start | bytes 847880 | tf_op jit(solution)/shard_map/ppermute | solution.py:371
  22.0 0.0 collective-permute-start.2
  22.0 0.0 collective-permute-done.4.zstrip
  22.0 0.0 collective-permute-done.3.edge
  22.0 1.7 %collective-permute-start.5 = (f32[47,4,128]{2,1,0:T(4,128)S(1)}, f32[47,4,128]{2,1,0:T(4,128)S(1)}, u32[]{:S(2)}, u32[]{:S(2)}) collective-permute-start(f32[47,4,128]{2,1,0:T(4,128)S(1)} %get-tuple-element.31), channel_id=1, source_target_pairs={{0,2},{2,4},{4,6},{6,8},{8,10},{10,12},{12,14},{14,0},{1,3},{3,5},... | collective-permute-start | bytes 288776 | tf_op jit(solution)/shard_map/ppermute | solution.py:378
  23.7 0.1 collective-permute-start.6
  23.9 1.6 %collective-permute-done.1.left = f32[138,4,128]{2,1,0:T(4,128)S(1)} collective-permute-done((f32[138,4,128]{2,1,0:T(4,128)S(1)}, f32[138,4,128]{2,1,0:T(4,128)S(1)}, u32[]{:S(2)}, u32[]{:S(2)}) %collective-permute-start.1) | collective-permute-done | bytes 282656 | tf_op jit(solution)/shard_map/ppermute | solution.py:371
  25.5 2.8 %collective-permute-done.2.right = f32[138,4,128]{2,1,0:T(4,128)S(1)} collective-permute-done((f32[138,4,128]{2,1,0:T(4,128)S(1)}, f32[138,4,128]{2,1,0:T(4,128)S(1)}, u32[]{:S(2)}, u32[]{:S(2)}) %collective-permute-start.2) | collective-permute-done | bytes 282656 | tf_op jit(solution)/shard_map/ppermute | solution.py:372
  28.3 3.4 %shard_map.71 = (f32[3,16,16,128]{3,2,1,0:T(8,128)}, f32[3,16,16,128]{3,2,1,0:T(8,128)}, f32[6,5,24,256]{3,2,1,0:T(8,128)S(1)}, f32[2,24,256]{2,1,0:T(8,128)S(1)}) custom-call(f32[2,8,128]{2,1,0:T(8,128)S(1)} %get-tuple-element.21.kerr, f32[3,16,16,128]{3,2,1,0:T(8,128)S(1)} %copy-done, f32[3,16,16,128]{3,2,1,0:T(8,128)S(1)} %copy-done.1, ...), custom_call_target="tpu_custom_call" | custom-call | tf_op jit(solution)/shard_map/pallas_call | solution.py:382
  31.7 0.0 collective-permute-done.5.left
  31.7 0.0 collective-permute-done.6.right
  31.7 0.1 shard_map.73
  31.8 0.0 collective-permute-done.7.mid
  31.8 2.4 %shard_map.74 = (f32[3,16,16,128]{3,2,1,0:T(8,128)}, f32[3,16,16,128]{3,2,1,0:T(8,128)}) custom-call(f32[6,5,24,256]{3,2,1,0:T(8,128)S(1)} %get-tuple-element.27.kept, f32[2,24,256]{2,1,0:T(8,128)S(1)} %get-tuple-element.28.cell, f32[44,2,8,128]{3,2,1,0:T(8,128)S(1)} %get-tuple-element.33.planes, ...), custom_call_target="tpu_custom_call", output_to_operand_aliasing={{0}: (5, {}), {1}: (6, {})} | custom-call | tf_op jit(solution)/shard_map/pallas_call | solution.py:399
  (3 shorter events, 0.0 us)
Async XLA Ops:
  0.6 1.1 %copy-start.1 = (f32[3,16,16,128]{3,2,1,0:T(8,128)S(1)}, f32[3,16,16,128]{3,2,1,0:T(8,128)}, u32[]{:S(2)}) copy-start(f32[3,16,16,128]{3,2,1,0:T(8,128)} %h.5) | copy-start | bytes 1179652
  1.7 8.3 %copy-start = (f32[3,16,16,128]{3,2,1,0:T(8,128)S(1)}, f32[3,16,16,128]{3,2,1,0:T(8,128)}, u32[]{:S(2)}) copy-start(f32[3,16,16,128]{3,2,1,0:T(8,128)} %e.5) | copy-start | bytes 1179652
  1.7 8.3 %copy-start.3 = (s32[16,128]{1,0:T(8,128)S(1)}, s32[16,128]{1,0:T(8,128)}, u32[]{:S(2)}) copy-start(s32[16,128]{1,0:T(8,128)} %material.1) | copy-start | bytes 24580
  1.9 20.0 %collective-permute-start.3 = (f32[88,4,128]{2,1,0:T(4,128)S(1)}, f32[88,4,128]{2,1,0:T(4,128)S(1)}, u32[]{:S(2)}, u32[]{:S(2)}) collective-permute-start(f32[88,4,128]{2,1,0:T(4,128)S(1)} %get-tuple-element.29), channel_id=1, source_target_pairs={{16,0},{32,16},{48,32},{64,48},{80,64},{96,80},{112,96},{128,112},... | collective-permute-start | bytes 540680 | tf_op jit(solution)/shard_map/ppermute | solution.py:357
  10.0 0.7 %copy-start.4 = (f32[2]{0:T(128)S(1)}, f32[2]{0:T(128)}, u32[]{:S(2)}) copy-start(f32[2]{0:T(128)} %param.9) | copy-start | bytes 28
  10.7 1.0 %copy-start.2 = (f32[4,2,8,16,128]{4,3,2,1,0:T(8,128)S(1)}, f32[4,2,8,16,128]{4,3,2,1,0:T(8,128)}, u32[]{:S(2)}) copy-start(f32[4,2,8,16,128]{4,3,2,1,0:T(8,128)} %aux.1) | copy-start | bytes 1572868
  12.2 7.4 %collective-permute-start = (f32[9,16,128]{2,1,0:T(8,128)S(1)}, f32[9,16,128]{2,1,0:T(8,128)S(1)}, u32[]{:S(2)}, u32[]{:S(2)}) collective-permute-start(f32[9,16,128]{2,1,0:T(8,128)S(1)} %get-tuple-element.24), channel_id=1, source_target_pairs={{0,1},{1,0},{2,3},{3,2},{4,5},{5,4},{6,7},{7,6},{8,9},{9,8},{10,11... | collective-permute-start | bytes 221192 | tf_op jit(solution)/shard_map/ppermute | solution.py:367
  13.0 9.0 %collective-permute-start.4 = (f32[3,16,128]{2,1,0:T(8,128)S(1)}, f32[3,16,128]{2,1,0:T(8,128)S(1)}, u32[]{:S(2)}, u32[]{:S(2)}) collective-permute-start(f32[3,16,128]{2,1,0:T(8,128)S(1)} %get-tuple-element.30), channel_id=1, source_target_pairs={{16,1},{17,0},{32,17},{33,16},{48,33},{49,32},{64,49},{65,48},{80,... | collective-permute-start | bytes 73736 | tf_op jit(solution)/shard_map/ppermute | solution.py:358
  15.6 16.1 %collective-permute-start.7 = (f32[44,8,128]{2,1,0:T(8,128)S(1)}, f32[44,8,128]{2,1,0:T(8,128)S(1)}, u32[]{:S(2)}, u32[]{:S(2)}) collective-permute-start(f32[44,8,128]{2,1,0:T(8,128)S(1)} %get-tuple-element.35), channel_id=1, source_target_pairs={{16,0},{32,16},{48,32},{64,48},{80,64},{96,80},{112,96},{128,112},... | collective-permute-start | bytes 540680 | tf_op jit(solution)/shard_map/ppermute | solution.py:359
  19.7 5.8 %collective-permute-start.1 = (f32[138,4,128]{2,1,0:T(4,128)S(1)}, f32[138,4,128]{2,1,0:T(4,128)S(1)}, u32[]{:S(2)}, u32[]{:S(2)}) collective-permute-start(f32[138,4,128]{2,1,0:T(4,128)S(1)} %get-tuple-element.25), channel_id=1, source_target_pairs={{0,2},{2,4},{4,6},{6,8},{8,10},{10,12},{12,14},{14,0},{1,3},{3,5},... | collective-permute-start | bytes 847880 | tf_op jit(solution)/shard_map/ppermute | solution.py:371
  22.0 6.3 %collective-permute-start.2 = (f32[138,4,128]{2,1,0:T(4,128)S(1)}, f32[138,4,128]{2,1,0:T(4,128)S(1)}, u32[]{:S(2)}, u32[]{:S(2)}) collective-permute-start(f32[138,4,128]{2,1,0:T(4,128)S(1)} %get-tuple-element.26), channel_id=1, source_target_pairs={{0,14},{2,0},{4,2},{6,4},{8,6},{10,8},{12,10},{14,12},{1,15},{3,1}... | collective-permute-start | bytes 847880 | tf_op jit(solution)/shard_map/ppermute | solution.py:372
  22.0 9.7 %collective-permute-start.5 = (f32[47,4,128]{2,1,0:T(4,128)S(1)}, f32[47,4,128]{2,1,0:T(4,128)S(1)}, u32[]{:S(2)}, u32[]{:S(2)}) collective-permute-start(f32[47,4,128]{2,1,0:T(4,128)S(1)} %get-tuple-element.31), channel_id=1, source_target_pairs={{0,2},{2,4},{4,6},{6,8},{8,10},{10,12},{12,14},{14,0},{1,3},{3,5},... | collective-permute-start | bytes 288776 | tf_op jit(solution)/shard_map/ppermute | solution.py:378
  23.7 8.0 %collective-permute-start.6 = (f32[47,4,128]{2,1,0:T(4,128)S(1)}, f32[47,4,128]{2,1,0:T(4,128)S(1)}, u32[]{:S(2)}, u32[]{:S(2)}) collective-permute-start(f32[47,4,128]{2,1,0:T(4,128)S(1)} %get-tuple-element.32), channel_id=1, source_target_pairs={{0,14},{2,0},{4,2},{6,4},{8,6},{10,8},{12,10},{14,12},{1,15},{3,1}... | collective-permute-start | bytes 288776 | tf_op jit(solution)/shard_map/ppermute | solution.py:379

commit v3 on v2

--- a/solution.py
+++ b/solution.py
@@ -94,7 +94,7 @@
     token[...] = jnp.zeros((8, LANES), F32)
 
 
-def strip_body(e, h, aux, material, kerr, token, ystrip, chosen, mat, kerrs, sem):
+def strip_body(e, h, aux, material, token, ystrip, chosen, mat, sem):
     at_front, _ = ends()
     copy = pltpu.make_async_copy(aux.at[:, pl.ds(jnp.where(at_front, 0, 1), 1)], chosen, sem)
     copy.start()
@@ -103,8 +103,6 @@
         ystrip[c] = strip([src[c % 3, z] for z in range(PLANES)])
     mat[...] = material[...].astype(F32)
     ystrip[FIELDS + 2] = strip([mat[...]])
-    for i in range(2):
-        kerrs[i] = jnp.broadcast_to(kerr[0:1, i : i + 1], (8, LANES))
     copy.wait()
     for j in range(2):
         ystrip[FIELDS + j] = strip([chosen[2 * j + k // PML, 0, k % PML] for k in range(16)])
@@ -131,7 +129,10 @@
         strips[j] = tall(zstrip[j], left[SENT + j], right[SENT + j])
 
 
-def rows_body(e, h, aux, mat, ystrip, to_left, to_right):
+def rows_body(e, h, aux, mat, ystrip, kerr, to_left, to_right, kerrs):
+    for i in range(2):
+        kerrs[i] = jnp.broadcast_to(kerr[0:1, i : i + 1], (8, LANES))
+
     def put(at, tile):
         to_left[at] = tile[0:4]
         to_right[at] = tile[12:16]
@@ -337,7 +338,16 @@
         send(0).wait()
 
 
-COST = {relay_body: pl.CostEstimate(flops=3_000_000_000, bytes_accessed=3_000_000_000, transcendentals=0)}
+def cost(figure):
+    return pl.CostEstimate(flops=figure, bytes_accessed=figure, transcendentals=0)
+
+
+COST = {
+    deep_body: cost(3_000_000_000),
+    strip_body: cost(3_000_000_000),
+    rows_body: cost(10_000_000_000),
+    relay_body: cost(1_800_000_000),
+}
 
 
 def shards(electric, magnetic, aux_state, material, kerr_strength):
@@ -358,16 +368,18 @@
     zs = lax.ppermute(zs, ("gz", "gy"), back_swap)
     mid = lax.ppermute(mid, "gz", back)
 
-    ys, aux, mat, kerr = call(
+    ys, aux, mat = call(
         strip_body,
-        [(GROUPS, ROWS, LANES), (4, 1, PML, ROWS, LANES), (ROWS, LANES), (2, 8, LANES)],
-        [VMEM, VMEM, HBM, VMEM, VMEM, VMEM],
+        [(GROUPS, ROWS, LANES), (4, 1, PML, ROWS, LANES), (ROWS, LANES)],
+        [VMEM, VMEM, HBM, VMEM, VMEM],
         [dma(())],
-    )(electric, magnetic, aux_state, material, kerr_strength[None], token)
+    )(electric, magnetic, aux_state, material, token)
     ys = lax.ppermute(ys, "gy", swap)
 
     rows = (TAKEN + GROUPS, 4, LANES)
-    my_first, my_last = call(rows_body, [rows, rows], [VMEM] * 5)(electric, magnetic, aux, mat, ys)
+    my_first, my_last, kerr = call(rows_body, [rows, rows, (2, 8, LANES)], [VMEM] * 6)(
+        electric, magnetic, aux, mat, ys, kerr_strength[None]
+    )
     from_left = lax.ppermute(my_last, "gx", to_right)
     from_right = lax.ppermute(my_first, "gx", to_left)
 

time: 34.4 us -> 33.8 us (0.983)
  the two profiles are of different devices: /device:TPU:25 before, /device:TPU:56 now
where the time goes in v3:
time: 33.8 us; the launch traced here: 33.6 us
  starting transfers between devices  20.8 us (62%)
  Pallas kernels  6.57 us (19%)
  waiting for transfers between devices  2.79 us (8%)
  local copies, waits for them, and re-layouts  2.72 us (8%)
  between operations  0.8 us (2%)
    ppermute x1, starting transfers between devices, shards(): edge = lax.ppermute(edge, 'gz', back)  8.38 us
    ppermute x1, starting transfers between devices, shards(): zs = lax.ppermute(zs, ('gz', 'gy'), back_swap)  3.82 us
    pallas_call x1, Pallas kernels, shards(): call(early_body, [part, part, (FIELDS, KEPT, TALL, WIDE), (2, TALL, WIDE)...  3.41 us
    ppermute x1, starting transfers between devices, shards(): from_right = lax.ppermute(my_first, 'gx', to_left)  2.94 us
    ppermute x1, starting transfers between devices, shards(): right = lax.ppermute(go_left, 'gx', to_left)  2.94 us
    ppermute x1, waiting for transfers between devices, shards(): mid = lax.ppermute(mid, 'gz', back)  2.77 us
    ppermute x1, starting transfers between devices, shards(): mid = lax.ppermute(mid, 'gz', back)  2.45 us
    pallas_call x1, Pallas kernels, shards(): call(late_body, [part, part], [VMEM] * 5 + [HBM, HBM], [pltpu.VMEM((FIELD...  2.4 us
  transfers between devices with their start and end apart: 8, of which 1 were waited for; matrix products, arithmetic and copies ran while one was open for 0% of the time, Pallas kernels for 11%

profile of v3, /device:TPU:56, one launch (start us, length us, event | category | flops | bytes accessed | tf_op | source)
XLA Modules:
  0.0 33.6 jit_solution(3649041315166575003)
XLA Ops:
  0.6 0.0 copy-start.1
  0.6 1.0 %slice.6.e = f32[3,8,16,128]{3,2,1,0:T(8,128)S(1)} slice(f32[3,16,16,128]{3,2,1,0:T(8,128)} %e.5), slice={[0:3], [0:8], [0:16], [0:128]} | slice | bytes 393216 | tf_op jit(solution)/shard_map/slice | solution.py:366
  1.6 0.1 copy-done.1
  1.7 0.0 copy-start
  1.7 0.0 copy-start.2
  1.8 0.0 copy-start.3
  1.8 0.2 shard_map.68
  1.9 0.8 %copy-done = f32[3,16,16,128]{3,2,1,0:T(8,128)S(1)} copy-done((f32[3,16,16,128]{3,2,1,0:T(8,128)S(1)}, f32[3,16,16,128]{3,2,1,0:T(8,128)}, u32[]{:S(2)}) %copy-start) | copy-done | bytes 393240
  2.7 0.2 copy-done.2
  2.9 0.4 %shard_map.69 = (f32[9,16,128]{2,1,0:T(8,128)S(1)}, f32[4,1,8,16,128]{4,3,2,1,0:T(8,128)S(1)}, f32[16,128]{1,0:T(8,128)S(1)}) custom-call(f32[3,16,16,128]{3,2,1,0:T(8,128)S(1)} %copy-done, f32[3,16,16,128]{3,2,1,0:T(8,128)S(1)} %copy-done.1, f32[4,2,8,16,128]{4,3,2,1,0:T(8,128)S(1)} %copy-done.2, s32[16,128]{1,0:T(8,128)S(1)} %copy-done.3, ...), custom_call_target="tpu_custom_call" | custom-call | flops 3000000000 | bytes 3000000000 | tf_op jit(solution)/shard_map/pallas_call | solution.py:371
  3.3 0.2 collective-permute-start
  3.5 8.4 %collective-permute-start.3 = (f32[88,4,128]{2,1,0:T(4,128)S(1)}, f32[88,4,128]{2,1,0:T(4,128)S(1)}, u32[]{:S(2)}, u32[]{:S(2)}) collective-permute-start(f32[88,4,128]{2,1,0:T(4,128)S(1)} %get-tuple-element.29), channel_id=1, source_target_pairs={{16,0},{32,16},{48,32},{64,48},{80,64},{96,80},{112,96},{128,112},... | collective-permute-start | bytes 540680 | tf_op jit(solution)/shard_map/ppermute | solution.py:367
  11.9 3.8 %collective-permute-start.4 = (f32[3,16,128]{2,1,0:T(8,128)S(1)}, f32[3,16,128]{2,1,0:T(8,128)S(1)}, u32[]{:S(2)}, u32[]{:S(2)}) collective-permute-start(f32[3,16,128]{2,1,0:T(8,128)S(1)} %get-tuple-element.30), channel_id=1, source_target_pairs={{16,1},{17,0},{32,17},{33,16},{48,33},{49,32},{64,49},{65,48},{80,... | collective-permute-start | bytes 73736 | tf_op jit(solution)/shard_map/ppermute | solution.py:368
  15.8 0.0 collective-permute-done.ystrip
  15.8 0.0 copy-start.4
  15.8 0.6 %copy-done.4 = f32[2]{0:T(128)S(1)} copy-done((f32[2]{0:T(128)S(1)}, f32[2]{0:T(128)}, u32[]{:S(2)}) %copy-start.4) | copy-done | bytes 32
  16.4 0.1 shard_map.70
  16.5 0.0 collective-permute-start.1
  16.5 2.9 %collective-permute-start.2 = (f32[138,4,128]{2,1,0:T(4,128)S(1)}, f32[138,4,128]{2,1,0:T(4,128)S(1)}, u32[]{:S(2)}, u32[]{:S(2)}) collective-permute-start(f32[138,4,128]{2,1,0:T(4,128)S(1)} %get-tuple-element.26), channel_id=1, source_target_pairs={{0,14},{2,0},{4,2},{6,4},{8,6},{10,8},{12,10},{14,12},{1,15},{3,1}... | collective-permute-start | bytes 847880 | tf_op jit(solution)/shard_map/ppermute | solution.py:384
  19.5 2.4 %collective-permute-start.7 = (f32[44,8,128]{2,1,0:T(8,128)S(1)}, f32[44,8,128]{2,1,0:T(8,128)S(1)}, u32[]{:S(2)}, u32[]{:S(2)}) collective-permute-start(f32[44,8,128]{2,1,0:T(8,128)S(1)} %get-tuple-element.35), channel_id=1, source_target_pairs={{16,0},{32,16},{48,32},{64,48},{80,64},{96,80},{112,96},{128,112},... | collective-permute-start | bytes 540680 | tf_op jit(solution)/shard_map/ppermute | solution.py:369
  21.9 0.0 collective-permute-done.4.zstrip
  21.9 0.0 collective-permute-done.3.edge
  22.0 0.0 collective-permute-start.5
  22.0 2.9 %collective-permute-start.6 = (f32[47,4,128]{2,1,0:T(4,128)S(1)}, f32[47,4,128]{2,1,0:T(4,128)S(1)}, u32[]{:S(2)}, u32[]{:S(2)}) collective-permute-start(f32[47,4,128]{2,1,0:T(4,128)S(1)} %get-tuple-element.32), channel_id=1, source_target_pairs={{0,14},{2,0},{4,2},{6,4},{8,6},{10,8},{12,10},{14,12},{1,15},{3,1}... | collective-permute-start | bytes 288776 | tf_op jit(solution)/shard_map/ppermute | solution.py:391
  24.9 0.0 collective-permute-done.1.left
  24.9 0.0 collective-permute-done.2.right
  24.9 3.4 %shard_map.71 = (f32[3,16,16,128]{3,2,1,0:T(8,128)}, f32[3,16,16,128]{3,2,1,0:T(8,128)}, f32[6,5,24,256]{3,2,1,0:T(8,128)S(1)}, f32[2,24,256]{2,1,0:T(8,128)S(1)}) custom-call(f32[2,8,128]{2,1,0:T(8,128)S(1)} %get-tuple-element.24.kerr, f32[3,16,16,128]{3,2,1,0:T(8,128)S(1)} %copy-done, f32[3,16,16,128]{3,2,1,0:T(8,128)S(1)} %copy-done.1, ...), custom_call_target="tpu_custom_call" | custom-call | tf_op jit(solution)/shard_map/pallas_call | solution.py:394
  28.4 0.0 collective-permute-done.5.left
  28.4 0.0 collective-permute-done.6.right
  28.4 0.1 shard_map.73
  28.4 2.8 %collective-permute-done.7.mid = f32[44,8,128]{2,1,0:T(8,128)S(1)} collective-permute-done((f32[44,8,128]{2,1,0:T(8,128)S(1)}, f32[44,8,128]{2,1,0:T(8,128)S(1)}, u32[]{:S(2)}, u32[]{:S(2)}) %collective-permute-start.7) | collective-permute-done | bytes 180256 | tf_op jit(solution)/shard_map/ppermute | solution.py:369
  31.2 2.4 %shard_map.74 = (f32[3,16,16,128]{3,2,1,0:T(8,128)}, f32[3,16,16,128]{3,2,1,0:T(8,128)}) custom-call(f32[6,5,24,256]{3,2,1,0:T(8,128)S(1)} %get-tuple-element.27.kept, f32[2,24,256]{2,1,0:T(8,128)S(1)} %get-tuple-element.28.cell, f32[44,2,8,128]{3,2,1,0:T(8,128)S(1)} %get-tuple-element.33.planes, ...), custom_call_target="tpu_custom_call", output_to_operand_aliasing={{0}: (5, {}), {1}: (6, {})} | custom-call | tf_op jit(solution)/shard_map/pallas_call | solution.py:411
  (3 shorter events, 0.0 us)
Async XLA Ops:
  0.6 1.1 %copy-start.1 = (f32[3,16,16,128]{3,2,1,0:T(8,128)S(1)}, f32[3,16,16,128]{3,2,1,0:T(8,128)}, u32[]{:S(2)}) copy-start(f32[3,16,16,128]{3,2,1,0:T(8,128)} %h.5) | copy-start | bytes 1179652
  1.7 1.0 %copy-start = (f32[3,16,16,128]{3,2,1,0:T(8,128)S(1)}, f32[3,16,16,128]{3,2,1,0:T(8,128)}, u32[]{:S(2)}) copy-start(f32[3,16,16,128]{3,2,1,0:T(8,128)} %e.5) | copy-start | bytes 1179652
  1.7 1.2 %copy-start.2 = (f32[4,2,8,16,128]{4,3,2,1,0:T(8,128)S(1)}, f32[4,2,8,16,128]{4,3,2,1,0:T(8,128)}, u32[]{:S(2)}) copy-start(f32[4,2,8,16,128]{4,3,2,1,0:T(8,128)} %aux.1) | copy-start | bytes 1572868
  1.8 1.1 %copy-start.3 = (s32[16,128]{1,0:T(8,128)S(1)}, s32[16,128]{1,0:T(8,128)}, u32[]{:S(2)}) copy-start(s32[16,128]{1,0:T(8,128)} %material.1) | copy-start | bytes 24580
  3.3 12.4 %collective-permute-start = (f32[9,16,128]{2,1,0:T(8,128)S(1)}, f32[9,16,128]{2,1,0:T(8,128)S(1)}, u32[]{:S(2)}, u32[]{:S(2)}) collective-permute-start(f32[9,16,128]{2,1,0:T(8,128)S(1)} %get-tuple-element.23), channel_id=1, source_target_pairs={{0,1},{1,0},{2,3},{3,2},{4,5},{5,4},{6,7},{7,6},{8,9},{9,8},{10,11... | collective-permute-start | bytes 221192 | tf_op jit(solution)/shard_map/ppermute | solution.py:377
  3.5 18.4 %collective-permute-start.3 = (f32[88,4,128]{2,1,0:T(4,128)S(1)}, f32[88,4,128]{2,1,0:T(4,128)S(1)}, u32[]{:S(2)}, u32[]{:S(2)}) collective-permute-start(f32[88,4,128]{2,1,0:T(4,128)S(1)} %get-tuple-element.29), channel_id=1, source_target_pairs={{16,0},{32,16},{48,32},{64,48},{80,64},{96,80},{112,96},{128,112},... | collective-permute-start | bytes 540680 | tf_op jit(solution)/shard_map/ppermute | solution.py:367
  11.9 10.0 %collective-permute-start.4 = (f32[3,16,128]{2,1,0:T(8,128)S(1)}, f32[3,16,128]{2,1,0:T(8,128)S(1)}, u32[]{:S(2)}, u32[]{:S(2)}) collective-permute-start(f32[3,16,128]{2,1,0:T(8,128)S(1)} %get-tuple-element.30), channel_id=1, source_target_pairs={{16,1},{17,0},{32,17},{33,16},{48,33},{49,32},{64,49},{65,48},{80,... | collective-permute-start | bytes 73736 | tf_op jit(solution)/shard_map/ppermute | solution.py:368
  15.8 0.7 %copy-start.4 = (f32[2]{0:T(128)S(1)}, f32[2]{0:T(128)}, u32[]{:S(2)}) copy-start(f32[2]{0:T(128)} %param.9) | copy-start | bytes 28
  16.5 8.4 %collective-permute-start.1 = (f32[138,4,128]{2,1,0:T(4,128)S(1)}, f32[138,4,128]{2,1,0:T(4,128)S(1)}, u32[]{:S(2)}, u32[]{:S(2)}) collective-permute-start(f32[138,4,128]{2,1,0:T(4,128)S(1)} %get-tuple-element.25), channel_id=1, source_target_pairs={{0,2},{2,4},{4,6},{6,8},{8,10},{10,12},{12,14},{14,0},{1,3},{3,5},... | collective-permute-start | bytes 847880 | tf_op jit(solution)/shard_map/ppermute | solution.py:383
  16.5 8.4 %collective-permute-start.2 = (f32[138,4,128]{2,1,0:T(4,128)S(1)}, f32[138,4,128]{2,1,0:T(4,128)S(1)}, u32[]{:S(2)}, u32[]{:S(2)}) collective-permute-start(f32[138,4,128]{2,1,0:T(4,128)S(1)} %get-tuple-element.26), channel_id=1, source_target_pairs={{0,14},{2,0},{4,2},{6,4},{8,6},{10,8},{12,10},{14,12},{1,15},{3,1}... | collective-permute-start | bytes 847880 | tf_op jit(solution)/shard_map/ppermute | solution.py:384
  19.5 11.8 %collective-permute-start.7 = (f32[44,8,128]{2,1,0:T(8,128)S(1)}, f32[44,8,128]{2,1,0:T(8,128)S(1)}, u32[]{:S(2)}, u32[]{:S(2)}) collective-permute-start(f32[44,8,128]{2,1,0:T(8,128)S(1)} %get-tuple-element.35), channel_id=1, source_target_pairs={{16,0},{32,16},{48,32},{64,48},{80,64},{96,80},{112,96},{128,112},... | collective-permute-start | bytes 540680 | tf_op jit(solution)/shard_map/ppermute | solution.py:369
  22.0 6.4 %collective-permute-start.5 = (f32[47,4,128]{2,1,0:T(4,128)S(1)}, f32[47,4,128]{2,1,0:T(4,128)S(1)}, u32[]{:S(2)}, u32[]{:S(2)}) collective-permute-start(f32[47,4,128]{2,1,0:T(4,128)S(1)} %get-tuple-element.31), channel_id=1, source_target_pairs={{0,2},{2,4},{4,6},{6,8},{8,10},{10,12},{12,14},{14,0},{1,3},{3,5},... | collective-permute-start | bytes 288776 | tf_op jit(solution)/shard_map/ppermute | solution.py:390
  22.0 6.4 %collective-permute-start.6 = (f32[47,4,128]{2,1,0:T(4,128)S(1)}, f32[47,4,128]{2,1,0:T(4,128)S(1)}, u32[]{:S(2)}, u32[]{:S(2)}) collective-permute-start(f32[47,4,128]{2,1,0:T(4,128)S(1)} %get-tuple-element.32), channel_id=1, source_target_pairs={{0,14},{2,0},{4,2},{6,4},{8,6},{10,8},{12,10},{14,12},{1,15},{3,1}... | collective-permute-start | bytes 288776 | tf_op jit(solution)/shard_map/ppermute | solution.py:391

commit v4 on v3

--- a/solution.py
+++ b/solution.py
@@ -112,7 +112,9 @@
     return jnp.concatenate([above, own, below], 0)
 
 
-def relay_body(edge, zstrip, to_left, to_right):
+def relay_body(edge, zstrip, kerr, to_left, to_right, kerrs):
+    for i in range(2):
+        kerrs[i] = jnp.broadcast_to(kerr[0:1, i : i + 1], (8, LANES))
     for at in range(SENT):
         to_left[at] = edge[at]
         to_right[at] = edge[SENT + at]
@@ -129,9 +131,7 @@
         strips[j] = tall(zstrip[j], left[SENT + j], right[SENT + j])
 
 
-def rows_body(e, h, aux, mat, ystrip, kerr, to_left, to_right, kerrs):
-    for i in range(2):
-        kerrs[i] = jnp.broadcast_to(kerr[0:1, i : i + 1], (8, LANES))
+def rows_body(e, h, aux, mat, ystrip, to_left, to_right):
 
     def put(at, tile):
         to_left[at] = tile[0:4]
@@ -346,7 +346,7 @@
     deep_body: cost(3_000_000_000),
     strip_body: cost(3_000_000_000),
     rows_body: cost(10_000_000_000),
-    relay_body: cost(1_800_000_000),
+    relay_body: cost(1_000_000_000),
 }
 
 
@@ -377,16 +377,14 @@
     ys = lax.ppermute(ys, "gy", swap)
 
     rows = (TAKEN + GROUPS, 4, LANES)
-    my_first, my_last, kerr = call(rows_body, [rows, rows, (2, 8, LANES)], [VMEM] * 6)(
-        electric, magnetic, aux, mat, ys, kerr_strength[None]
-    )
+    my_first, my_last = call(rows_body, [rows, rows], [VMEM] * 5)(electric, magnetic, aux, mat, ys)
     from_left = lax.ppermute(my_last, "gx", to_right)
     from_right = lax.ppermute(my_first, "gx", to_left)
 
     relayed = (SENT + 3, 4, LANES)
-    go_left, go_right = call(
-        relay_body, [relayed, relayed], [VMEM] * 2
-    )(edge, zs)
+    go_left, go_right, kerr = call(
+        relay_body, [relayed, relayed, (2, 8, LANES)], [VMEM] * 3
+    )(edge, zs, kerr_strength[None])
     left = lax.ppermute(go_right, "gx", to_right)
     right = lax.ppermute(go_left, "gx", to_left)
 

time: 33.8 us -> 33 us (0.976)
  waiting for transfers between devices: 2.79 us -> 1.52 us
  starting transfers between devices: 20.8 us -> 21.7 us
  local copies, waits for them, and re-layouts: 2.72 us -> 2.07 us
    ppermute x1, waiting for transfers between devices: 2.77 us -> 1.5 us  [shards(): mid = lax.ppermute(mid, 'gz', back)]
    ppermute x1, starting transfers between devices: 2.45 us -> 3.39 us  [shards(): mid = lax.ppermute(mid, 'gz', back)]
    unnamed x10, local copies, waits for them, and re-layouts: 1.71 us -> 1.06 us
where the time goes in v4:
time: 33 us; the launch traced here: 32.8 us
  starting transfers between devices  21.7 us (66%)
  Pallas kernels  6.69 us (20%)
  local copies, waits for them, and re-layouts  2.07 us (6%)
  waiting for transfers between devices  1.52 us (5%)
  between operations  0.79 us (2%)
    ppermute x1, starting transfers between devices, shards(): edge = lax.ppermute(edge, 'gz', back)  8.38 us
    ppermute x1, starting transfers between devices, shards(): zs = lax.ppermute(zs, ('gz', 'gy'), back_swap)  3.8 us
    pallas_call x1, Pallas kernels, shards(): call(early_body, [part, part, (FIELDS, KEPT, TALL, WIDE), (2, TALL, WIDE)...  3.46 us
    ppermute x1, starting transfers between devices, shards(): mid = lax.ppermute(mid, 'gz', back)  3.39 us
    ppermute x1, starting transfers between devices, shards(): right = lax.ppermute(go_left, 'gx', to_left)  2.95 us
    ppermute x1, starting transfers between devices, shards(): from_right = lax.ppermute(my_first, 'gx', to_left)  2.94 us
    pallas_call x1, Pallas kernels, shards(): call(late_body, [part, part], [VMEM] * 5 + [HBM, HBM], [pltpu.VMEM((FIELD...  2.43 us
    ppermute x1, waiting for transfers between devices, shards(): mid = lax.ppermute(mid, 'gz', back)  1.5 us
  transfers between devices with their start and end apart: 8, of which 1 were waited for; matrix products, arithmetic and copies ran while one was open for 0% of the time, Pallas kernels for 11%

profile of v4, /device:TPU:56, one launch (start us, length us, event | category | flops | bytes accessed | tf_op | source)
XLA Modules:
  0.0 32.8 jit_solution(6698810281221603127)
XLA Ops:
  0.6 1.0 %slice.6.e = f32[3,8,16,128]{3,2,1,0:T(8,128)S(1)} slice(f32[3,16,16,128]{3,2,1,0:T(8,128)} %e.5), slice={[0:3], [0:8], [0:16], [0:128]} | slice | bytes 393216 | tf_op jit(solution)/shard_map/slice | solution.py:366
  1.6 0.1 copy-done.1
  1.7 0.0 copy-start
  1.7 0.0 copy-start.2
  1.8 0.0 copy-start.3
  1.8 0.2 shard_map.68
  1.9 0.8 %copy-done = f32[3,16,16,128]{3,2,1,0:T(8,128)S(1)} copy-done((f32[3,16,16,128]{3,2,1,0:T(8,128)S(1)}, f32[3,16,16,128]{3,2,1,0:T(8,128)}, u32[]{:S(2)}) %copy-start) | copy-done | bytes 393240
  2.7 0.2 copy-done.2
  2.9 0.0 copy-done.3
  2.9 0.4 %shard_map.70 = (f32[9,16,128]{2,1,0:T(8,128)S(1)}, f32[4,1,8,16,128]{4,3,2,1,0:T(8,128)S(1)}, f32[16,128]{1,0:T(8,128)S(1)}) custom-call(f32[3,16,16,128]{3,2,1,0:T(8,128)S(1)} %copy-done, f32[3,16,16,128]{3,2,1,0:T(8,128)S(1)} %copy-done.1, f32[4,2,8,16,128]{4,3,2,1,0:T(8,128)S(1)} %copy-done.2, s32[16,128]{1,0:T(8,128)S(1)} %copy-done.3, ...), custom_call_target="tpu_custom_call" | custom-call | flops 3000000000 | bytes 3000000000 | tf_op jit(solution)/shard_map/pallas_call | solution.py:371
  3.3 0.2 collective-permute-start.2
  3.5 8.4 %collective-permute-start = (f32[88,4,128]{2,1,0:T(4,128)S(1)}, f32[88,4,128]{2,1,0:T(4,128)S(1)}, u32[]{:S(2)}, u32[]{:S(2)}) collective-permute-start(f32[88,4,128]{2,1,0:T(4,128)S(1)} %get-tuple-element.20), channel_id=1, source_target_pairs={{16,0},{32,16},{48,32},{64,48},{80,64},{96,80},{112,96},{128,112},... | collective-permute-start | bytes 540680 | tf_op jit(solution)/shard_map/ppermute | solution.py:367
  11.9 0.0 collective-permute-done.2.ystrip
  11.9 0.1 shard_map.71
  12.0 0.0 collective-permute-start.3
  12.0 2.9 %collective-permute-start.4 = (f32[138,4,128]{2,1,0:T(4,128)S(1)}, f32[138,4,128]{2,1,0:T(4,128)S(1)}, u32[]{:S(2)}, u32[]{:S(2)}) collective-permute-start(f32[138,4,128]{2,1,0:T(4,128)S(1)} %get-tuple-element.28), channel_id=1, source_target_pairs={{0,14},{2,0},{4,2},{6,4},{8,6},{10,8},{12,10},{14,12},{1,15},{3,1}... | collective-permute-start | bytes 847880 | tf_op jit(solution)/shard_map/ppermute | solution.py:382
  15.0 3.8 %collective-permute-start.1 = (f32[3,16,128]{2,1,0:T(8,128)S(1)}, f32[3,16,128]{2,1,0:T(8,128)S(1)}, u32[]{:S(2)}, u32[]{:S(2)}) collective-permute-start(f32[3,16,128]{2,1,0:T(8,128)S(1)} %get-tuple-element.21), channel_id=1, source_target_pairs={{16,1},{17,0},{32,17},{33,16},{48,33},{49,32},{64,49},{65,48},{80,... | collective-permute-start | bytes 73736 | tf_op jit(solution)/shard_map/ppermute | solution.py:368
  18.8 0.0 copy-start.4
  18.8 3.4 %collective-permute-start.7 = (f32[44,8,128]{2,1,0:T(8,128)S(1)}, f32[44,8,128]{2,1,0:T(8,128)S(1)}, u32[]{:S(2)}, u32[]{:S(2)}) collective-permute-start(f32[44,8,128]{2,1,0:T(8,128)S(1)} %get-tuple-element.35), channel_id=1, source_target_pairs={{16,0},{32,16},{48,32},{64,48},{80,64},{96,80},{112,96},{128,112},... | collective-permute-start | bytes 540680 | tf_op jit(solution)/shard_map/ppermute | solution.py:369
  22.2 0.0 collective-permute-done.1.zstrip
  22.2 0.0 collective-permute-done.edge
  22.2 0.1 shard_map.69
  22.3 0.0 collective-permute-start.5
  22.3 3.0 %collective-permute-start.6 = (f32[47,4,128]{2,1,0:T(4,128)S(1)}, f32[47,4,128]{2,1,0:T(4,128)S(1)}, u32[]{:S(2)}, u32[]{:S(2)}) collective-permute-start(f32[47,4,128]{2,1,0:T(4,128)S(1)} %get-tuple-element.32), channel_id=1, source_target_pairs={{0,14},{2,0},{4,2},{6,4},{8,6},{10,8},{12,10},{14,12},{1,15},{3,1}... | collective-permute-start | bytes 288776 | tf_op jit(solution)/shard_map/ppermute | solution.py:389
  25.3 0.0 collective-permute-done.3.left
  25.3 0.0 collective-permute-done.4.right
  25.3 3.5 %shard_map.72 = (f32[3,16,16,128]{3,2,1,0:T(8,128)}, f32[3,16,16,128]{3,2,1,0:T(8,128)}, f32[6,5,24,256]{3,2,1,0:T(8,128)S(1)}, f32[2,24,256]{2,1,0:T(8,128)S(1)}) custom-call(f32[2,8,128]{2,1,0:T(8,128)S(1)} %get-tuple-element.22.kerr, f32[3,16,16,128]{3,2,1,0:T(8,128)S(1)} %copy-done, f32[3,16,16,128]{3,2,1,0:T(8,128)S(1)} %copy-done.1, ...), custom_call_target="tpu_custom_call" | custom-call | tf_op jit(solution)/shard_map/pallas_call | solution.py:392
  28.7 0.0 collective-permute-done.5.left
  28.8 0.0 collective-permute-done.6.right
  28.8 0.1 shard_map.73
  28.8 1.5 %collective-permute-done.7.mid = f32[44,8,128]{2,1,0:T(8,128)S(1)} collective-permute-done((f32[44,8,128]{2,1,0:T(8,128)S(1)}, f32[44,8,128]{2,1,0:T(8,128)S(1)}, u32[]{:S(2)}, u32[]{:S(2)}) %collective-permute-start.7) | collective-permute-done | bytes 180256 | tf_op jit(solution)/shard_map/ppermute | solution.py:369
  30.3 2.4 %shard_map.74 = (f32[3,16,16,128]{3,2,1,0:T(8,128)}, f32[3,16,16,128]{3,2,1,0:T(8,128)}) custom-call(f32[6,5,24,256]{3,2,1,0:T(8,128)S(1)} %get-tuple-element.29.kept, f32[2,24,256]{2,1,0:T(8,128)S(1)} %get-tuple-element.30.cell, f32[44,2,8,128]{3,2,1,0:T(8,128)S(1)} %get-tuple-element.33.planes, ...), custom_call_target="tpu_custom_call", output_to_operand_aliasing={{0}: (5, {}), {1}: (6, {})} | custom-call | tf_op jit(solution)/shard_map/pallas_call | solution.py:409
  (3 shorter events, 0.0 us)
Async XLA Ops:
  0.6 1.1 %copy-start.1 = (f32[3,16,16,128]{3,2,1,0:T(8,128)S(1)}, f32[3,16,16,128]{3,2,1,0:T(8,128)}, u32[]{:S(2)}) copy-start(f32[3,16,16,128]{3,2,1,0:T(8,128)} %h.5) | copy-start | bytes 1179652
  1.7 1.0 %copy-start = (f32[3,16,16,128]{3,2,1,0:T(8,128)S(1)}, f32[3,16,16,128]{3,2,1,0:T(8,128)}, u32[]{:S(2)}) copy-start(f32[3,16,16,128]{3,2,1,0:T(8,128)} %e.5) | copy-start | bytes 1179652
  1.7 1.2 %copy-start.2 = (f32[4,2,8,16,128]{4,3,2,1,0:T(8,128)S(1)}, f32[4,2,8,16,128]{4,3,2,1,0:T(8,128)}, u32[]{:S(2)}) copy-start(f32[4,2,8,16,128]{4,3,2,1,0:T(8,128)} %aux.1) | copy-start | bytes 1572868
  1.8 1.1 %copy-start.3 = (s32[16,128]{1,0:T(8,128)S(1)}, s32[16,128]{1,0:T(8,128)}, u32[]{:S(2)}) copy-start(s32[16,128]{1,0:T(8,128)} %material.1) | copy-start | bytes 24580
  3.3 8.6 %collective-permute-start.2 = (f32[9,16,128]{2,1,0:T(8,128)S(1)}, f32[9,16,128]{2,1,0:T(8,128)S(1)}, u32[]{:S(2)}, u32[]{:S(2)}) collective-permute-start(f32[9,16,128]{2,1,0:T(8,128)S(1)} %get-tuple-element.26), channel_id=1, source_target_pairs={{0,1},{1,0},{2,3},{3,2},{4,5},{5,4},{6,7},{7,6},{8,9},{9,8},{10,11... | collective-permute-start | bytes 221192 | tf_op jit(solution)/shard_map/ppermute | solution.py:377
  3.5 18.7 %collective-permute-start = (f32[88,4,128]{2,1,0:T(4,128)S(1)}, f32[88,4,128]{2,1,0:T(4,128)S(1)}, u32[]{:S(2)}, u32[]{:S(2)}) collective-permute-start(f32[88,4,128]{2,1,0:T(4,128)S(1)} %get-tuple-element.20), channel_id=1, source_target_pairs={{16,0},{32,16},{48,32},{64,48},{80,64},{96,80},{112,96},{128,112},... | collective-permute-start | bytes 540680 | tf_op jit(solution)/shard_map/ppermute | solution.py:367
  12.0 13.3 %collective-permute-start.3 = (f32[138,4,128]{2,1,0:T(4,128)S(1)}, f32[138,4,128]{2,1,0:T(4,128)S(1)}, u32[]{:S(2)}, u32[]{:S(2)}) collective-permute-start(f32[138,4,128]{2,1,0:T(4,128)S(1)} %get-tuple-element.27), channel_id=1, source_target_pairs={{0,2},{2,4},{4,6},{6,8},{8,10},{10,12},{12,14},{14,0},{1,3},{3,5},... | collective-permute-start | bytes 847880 | tf_op jit(solution)/shard_map/ppermute | solution.py:381
  12.0 13.2 %collective-permute-start.4 = (f32[138,4,128]{2,1,0:T(4,128)S(1)}, f32[138,4,128]{2,1,0:T(4,128)S(1)}, u32[]{:S(2)}, u32[]{:S(2)}) collective-permute-start(f32[138,4,128]{2,1,0:T(4,128)S(1)} %get-tuple-element.28), channel_id=1, source_target_pairs={{0,14},{2,0},{4,2},{6,4},{8,6},{10,8},{12,10},{14,12},{1,15},{3,1}... | collective-permute-start | bytes 847880 | tf_op jit(solution)/shard_map/ppermute | solution.py:382
  15.0 7.2 %collective-permute-start.1 = (f32[3,16,128]{2,1,0:T(8,128)S(1)}, f32[3,16,128]{2,1,0:T(8,128)S(1)}, u32[]{:S(2)}, u32[]{:S(2)}) collective-permute-start(f32[3,16,128]{2,1,0:T(8,128)S(1)} %get-tuple-element.21), channel_id=1, source_target_pairs={{16,1},{17,0},{32,17},{33,16},{48,33},{49,32},{64,49},{65,48},{80,... | collective-permute-start | bytes 73736 | tf_op jit(solution)/shard_map/ppermute | solution.py:368
  18.8 3.4 %copy-start.4 = (f32[2]{0:T(128)S(1)}, f32[2]{0:T(128)}, u32[]{:S(2)}) copy-start(f32[2]{0:T(128)} %param.9) | copy-start | bytes 28
  18.8 11.5 %collective-permute-start.7 = (f32[44,8,128]{2,1,0:T(8,128)S(1)}, f32[44,8,128]{2,1,0:T(8,128)S(1)}, u32[]{:S(2)}, u32[]{:S(2)}) collective-permute-start(f32[44,8,128]{2,1,0:T(8,128)S(1)} %get-tuple-element.35), channel_id=1, source_target_pairs={{16,0},{32,16},{48,32},{64,48},{80,64},{96,80},{112,96},{128,112},... | collective-permute-start | bytes 540680 | tf_op jit(solution)/shard_map/ppermute | solution.py:369
  22.3 6.4 %collective-permute-start.5 = (f32[47,4,128]{2,1,0:T(4,128)S(1)}, f32[47,4,128]{2,1,0:T(4,128)S(1)}, u32[]{:S(2)}, u32[]{:S(2)}) collective-permute-start(f32[47,4,128]{2,1,0:T(4,128)S(1)} %get-tuple-element.31), channel_id=1, source_target_pairs={{0,2},{2,4},{4,6},{6,8},{8,10},{10,12},{12,14},{14,0},{1,3},{3,5},... | collective-permute-start | bytes 288776 | tf_op jit(solution)/shard_map/ppermute | solution.py:388
  22.3 6.4 %collective-permute-start.6 = (f32[47,4,128]{2,1,0:T(4,128)S(1)}, f32[47,4,128]{2,1,0:T(4,128)S(1)}, u32[]{:S(2)}, u32[]{:S(2)}) collective-permute-start(f32[47,4,128]{2,1,0:T(4,128)S(1)} %get-tuple-element.32), channel_id=1, source_target_pairs={{0,14},{2,0},{4,2},{6,4},{8,6},{10,8},{12,10},{14,12},{1,15},{3,1}... | collective-permute-start | bytes 288776 | tf_op jit(solution)/shard_map/ppermute | solution.py:389

commit v5 on v4

--- a/solution.py
+++ b/solution.py
@@ -295,7 +295,6 @@
 
 def late_body(kept, cell, planes, strips, mid, old_e, old_h, out_e, out_h, f, done, sems):
     base = PLANES - KEPT
-    span = pl.ds(PLANES // 2, PLANES // 2)
 
     @pl.when(jnp.logical_not(ends()[1]))
     def _():
@@ -320,9 +319,12 @@
                 f[c, p - base] = value
             made.add((c, p))
 
-        def send(i):
+        def send(i, part):
+            size = PLANES // 4
             return pltpu.make_async_copy(
-                done.at[pl.ds(3 * i, 3)], (out_e, out_h)[i].at[:, span], sems.at[i]
+                done.at[pl.ds(3 * i, 3), pl.ds(part * size, size)],
+                (out_e, out_h)[i].at[:, pl.ds(PLANES // 2 + part * size, size)],
+                sems.at[2 * i + part],
             )
 
         for s in range(1, STEPS + 1):
@@ -330,12 +332,16 @@
             for p in window:
                 magnetic_plane(read, write, p)
             if s == STEPS:
-                send(1).start()
+                send(1, 0).start()
+                send(1, 1).start()
             for p in window:
                 electric_plane(read, write, cell, p)
-        send(0).start()
-        send(1).wait()
-        send(0).wait()
+                if s == STEPS and p == window[DEEP // 2 - 1]:
+                    send(0, 0).start()
+        send(0, 1).start()
+        for i in (1, 0):
+            for part in range(2):
+                send(i, part).wait()
 
 
 def cost(figure):
@@ -413,7 +419,7 @@
         [
             pltpu.VMEM((FIELDS, KEPT + DEEP, TALL, WIDE), F32),
             pltpu.VMEM((FIELDS, PLANES // 2, ROWS, LANES), F32),
-            dma((2,)),
+            dma((4,)),
         ],
         out_specs=[HBM, HBM],
         input_output_aliases={5: 0, 6: 1},

time: 33 us -> 32.9 us (level)
  no operation moved by 1% of the time
where the time goes in v5:
time: 32.9 us; the launch traced here: 32.7 us
  starting transfers between devices  21.7 us (66%)
  Pallas kernels  6.67 us (20%)
  local copies, waits for them, and re-layouts  2.07 us (6%)
  waiting for transfers between devices  1.52 us (5%)
  between operations  0.79 us (2%)
    ppermute x1, starting transfers between devices, shards(): edge = lax.ppermute(edge, 'gz', back)  8.38 us
    ppermute x1, starting transfers between devices, shards(): zs = lax.ppermute(zs, ('gz', 'gy'), back_swap)  3.8 us
    pallas_call x1, Pallas kernels, shards(): call(early_body, [part, part, (FIELDS, KEPT, TALL, WIDE), (2, TALL, WIDE)...  3.46 us
    ppermute x1, starting transfers between devices, shards(): mid = lax.ppermute(mid, 'gz', back)  3.39 us
    ppermute x1, starting transfers between devices, shards(): right = lax.ppermute(go_left, 'gx', to_left)  2.95 us
    ppermute x1, starting transfers between devices, shards(): from_right = lax.ppermute(my_first, 'gx', to_left)  2.94 us
    pallas_call x1, Pallas kernels, shards(): call(late_body, [part, part], [VMEM] * 5 + [HBM, HBM], [pltpu.VMEM((FIELD...  2.41 us
    ppermute x1, waiting for transfers between devices, shards(): mid = lax.ppermute(mid, 'gz', back)  1.5 us
  transfers between devices with their start and end apart: 8, of which 1 were waited for; matrix products, arithmetic and copies ran while one was open for 0% of the time, Pallas kernels for 11%

profile of v5, /device:TPU:56, one launch (start us, length us, event | category | flops | bytes accessed | tf_op | source)
XLA Modules:
  0.0 32.7 jit_solution(11501467458476738461)
XLA Ops:
  0.6 1.0 %slice.6.e = f32[3,8,16,128]{3,2,1,0:T(8,128)S(1)} slice(f32[3,16,16,128]{3,2,1,0:T(8,128)} %e.5), slice={[0:3], [0:8], [0:16], [0:128]} | slice | bytes 393216 | tf_op jit(solution)/shard_map/slice | solution.py:372
  1.6 0.1 copy-done.1
  1.7 0.0 copy-start
  1.7 0.0 copy-start.2
  1.8 0.0 copy-start.3
  1.8 0.2 shard_map.68
  1.9 0.8 %copy-done = f32[3,16,16,128]{3,2,1,0:T(8,128)S(1)} copy-done((f32[3,16,16,128]{3,2,1,0:T(8,128)S(1)}, f32[3,16,16,128]{3,2,1,0:T(8,128)}, u32[]{:S(2)}) %copy-start) | copy-done | bytes 393240
  2.7 0.2 copy-done.2
  2.9 0.0 copy-done.3
  2.9 0.4 %shard_map.70 = (f32[9,16,128]{2,1,0:T(8,128)S(1)}, f32[4,1,8,16,128]{4,3,2,1,0:T(8,128)S(1)}, f32[16,128]{1,0:T(8,128)S(1)}) custom-call(f32[3,16,16,128]{3,2,1,0:T(8,128)S(1)} %copy-done, f32[3,16,16,128]{3,2,1,0:T(8,128)S(1)} %copy-done.1, f32[4,2,8,16,128]{4,3,2,1,0:T(8,128)S(1)} %copy-done.2, s32[16,128]{1,0:T(8,128)S(1)} %copy-done.3, ...), custom_call_target="tpu_custom_call" | custom-call | flops 3000000000 | bytes 3000000000 | tf_op jit(solution)/shard_map/pallas_call | solution.py:377
  3.3 0.2 collective-permute-start.2
  3.5 8.4 %collective-permute-start = (f32[88,4,128]{2,1,0:T(4,128)S(1)}, f32[88,4,128]{2,1,0:T(4,128)S(1)}, u32[]{:S(2)}, u32[]{:S(2)}) collective-permute-start(f32[88,4,128]{2,1,0:T(4,128)S(1)} %get-tuple-element.20), channel_id=1, source_target_pairs={{16,0},{32,16},{48,32},{64,48},{80,64},{96,80},{112,96},{128,112},... | collective-permute-start | bytes 540680 | tf_op jit(solution)/shard_map/ppermute | solution.py:373
  11.9 0.0 collective-permute-done.2.ystrip
  11.9 0.1 shard_map.71
  12.0 0.0 collective-permute-start.3
  12.0 2.9 %collective-permute-start.4 = (f32[138,4,128]{2,1,0:T(4,128)S(1)}, f32[138,4,128]{2,1,0:T(4,128)S(1)}, u32[]{:S(2)}, u32[]{:S(2)}) collective-permute-start(f32[138,4,128]{2,1,0:T(4,128)S(1)} %get-tuple-element.28), channel_id=1, source_target_pairs={{0,14},{2,0},{4,2},{6,4},{8,6},{10,8},{12,10},{14,12},{1,15},{3,1}... | collective-permute-start | bytes 847880 | tf_op jit(solution)/shard_map/ppermute | solution.py:388
  15.0 3.8 %collective-permute-start.1 = (f32[3,16,128]{2,1,0:T(8,128)S(1)}, f32[3,16,128]{2,1,0:T(8,128)S(1)}, u32[]{:S(2)}, u32[]{:S(2)}) collective-permute-start(f32[3,16,128]{2,1,0:T(8,128)S(1)} %get-tuple-element.21), channel_id=1, source_target_pairs={{16,1},{17,0},{32,17},{33,16},{48,33},{49,32},{64,49},{65,48},{80,... | collective-permute-start | bytes 73736 | tf_op jit(solution)/shard_map/ppermute | solution.py:374
  18.8 0.0 copy-start.4
  18.8 3.4 %collective-permute-start.7 = (f32[44,8,128]{2,1,0:T(8,128)S(1)}, f32[44,8,128]{2,1,0:T(8,128)S(1)}, u32[]{:S(2)}, u32[]{:S(2)}) collective-permute-start(f32[44,8,128]{2,1,0:T(8,128)S(1)} %get-tuple-element.35), channel_id=1, source_target_pairs={{16,0},{32,16},{48,32},{64,48},{80,64},{96,80},{112,96},{128,112},... | collective-permute-start | bytes 540680 | tf_op jit(solution)/shard_map/ppermute | solution.py:375
  22.2 0.0 collective-permute-done.1.zstrip
  22.2 0.0 collective-permute-done.edge
  22.2 0.1 shard_map.69
  22.3 0.0 collective-permute-start.5
  22.3 3.0 %collective-permute-start.6 = (f32[47,4,128]{2,1,0:T(4,128)S(1)}, f32[47,4,128]{2,1,0:T(4,128)S(1)}, u32[]{:S(2)}, u32[]{:S(2)}) collective-permute-start(f32[47,4,128]{2,1,0:T(4,128)S(1)} %get-tuple-element.32), channel_id=1, source_target_pairs={{0,14},{2,0},{4,2},{6,4},{8,6},{10,8},{12,10},{14,12},{1,15},{3,1}... | collective-permute-start | bytes 288776 | tf_op jit(solution)/shard_map/ppermute | solution.py:395
  25.3 0.0 collective-permute-done.3.left
  25.3 0.0 collective-permute-done.4.right
  25.3 3.5 %shard_map.72 = (f32[3,16,16,128]{3,2,1,0:T(8,128)}, f32[3,16,16,128]{3,2,1,0:T(8,128)}, f32[6,5,24,256]{3,2,1,0:T(8,128)S(1)}, f32[2,24,256]{2,1,0:T(8,128)S(1)}) custom-call(f32[2,8,128]{2,1,0:T(8,128)S(1)} %get-tuple-element.22.kerr, f32[3,16,16,128]{3,2,1,0:T(8,128)S(1)} %copy-done, f32[3,16,16,128]{3,2,1,0:T(8,128)S(1)} %copy-done.1, ...), custom_call_target="tpu_custom_call" | custom-call | tf_op jit(solution)/shard_map/pallas_call | solution.py:398
  28.7 0.0 collective-permute-done.5.left
  28.8 0.0 collective-permute-done.6.right
  28.8 0.1 shard_map.73
  28.8 1.5 %collective-permute-done.7.mid = f32[44,8,128]{2,1,0:T(8,128)S(1)} collective-permute-done((f32[44,8,128]{2,1,0:T(8,128)S(1)}, f32[44,8,128]{2,1,0:T(8,128)S(1)}, u32[]{:S(2)}, u32[]{:S(2)}) %collective-permute-start.7) | collective-permute-done | bytes 180256 | tf_op jit(solution)/shard_map/ppermute | solution.py:375
  30.3 2.4 %shard_map.74 = (f32[3,16,16,128]{3,2,1,0:T(8,128)}, f32[3,16,16,128]{3,2,1,0:T(8,128)}) custom-call(f32[6,5,24,256]{3,2,1,0:T(8,128)S(1)} %get-tuple-element.29.kept, f32[2,24,256]{2,1,0:T(8,128)S(1)} %get-tuple-element.30.cell, f32[44,2,8,128]{3,2,1,0:T(8,128)S(1)} %get-tuple-element.33.planes, ...), custom_call_target="tpu_custom_call", output_to_operand_aliasing={{0}: (5, {}), {1}: (6, {})} | custom-call | tf_op jit(solution)/shard_map/pallas_call | solution.py:415
  (3 shorter events, 0.0 us)
Async XLA Ops:
  0.6 1.1 %copy-start.1 = (f32[3,16,16,128]{3,2,1,0:T(8,128)S(1)}, f32[3,16,16,128]{3,2,1,0:T(8,128)}, u32[]{:S(2)}) copy-start(f32[3,16,16,128]{3,2,1,0:T(8,128)} %h.5) | copy-start | bytes 1179652
  1.7 1.0 %copy-start = (f32[3,16,16,128]{3,2,1,0:T(8,128)S(1)}, f32[3,16,16,128]{3,2,1,0:T(8,128)}, u32[]{:S(2)}) copy-start(f32[3,16,16,128]{3,2,1,0:T(8,128)} %e.5) | copy-start | bytes 1179652
  1.7 1.2 %copy-start.2 = (f32[4,2,8,16,128]{4,3,2,1,0:T(8,128)S(1)}, f32[4,2,8,16,128]{4,3,2,1,0:T(8,128)}, u32[]{:S(2)}) copy-start(f32[4,2,8,16,128]{4,3,2,1,0:T(8,128)} %aux.1) | copy-start | bytes 1572868
  1.8 1.1 %copy-start.3 = (s32[16,128]{1,0:T(8,128)S(1)}, s32[16,128]{1,0:T(8,128)}, u32[]{:S(2)}) copy-start(s32[16,128]{1,0:T(8,128)} %material.1) | copy-start | bytes 24580
  3.3 8.6 %collective-permute-start.2 = (f32[9,16,128]{2,1,0:T(8,128)S(1)}, f32[9,16,128]{2,1,0:T(8,128)S(1)}, u32[]{:S(2)}, u32[]{:S(2)}) collective-permute-start(f32[9,16,128]{2,1,0:T(8,128)S(1)} %get-tuple-element.26), channel_id=1, source_target_pairs={{0,1},{1,0},{2,3},{3,2},{4,5},{5,4},{6,7},{7,6},{8,9},{9,8},{10,11... | collective-permute-start | bytes 221192 | tf_op jit(solution)/shard_map/ppermute | solution.py:383
  3.5 18.7 %collective-permute-start = (f32[88,4,128]{2,1,0:T(4,128)S(1)}, f32[88,4,128]{2,1,0:T(4,128)S(1)}, u32[]{:S(2)}, u32[]{:S(2)}) collective-permute-start(f32[88,4,128]{2,1,0:T(4,128)S(1)} %get-tuple-element.20), channel_id=1, source_target_pairs={{16,0},{32,16},{48,32},{64,48},{80,64},{96,80},{112,96},{128,112},... | collective-permute-start | bytes 540680 | tf_op jit(solution)/shard_map/ppermute | solution.py:373
  12.0 13.3 %collective-permute-start.3 = (f32[138,4,128]{2,1,0:T(4,128)S(1)}, f32[138,4,128]{2,1,0:T(4,128)S(1)}, u32[]{:S(2)}, u32[]{:S(2)}) collective-permute-start(f32[138,4,128]{2,1,0:T(4,128)S(1)} %get-tuple-element.27), channel_id=1, source_target_pairs={{0,2},{2,4},{4,6},{6,8},{8,10},{10,12},{12,14},{14,0},{1,3},{3,5},... | collective-permute-start | bytes 847880 | tf_op jit(solution)/shard_map/ppermute | solution.py:387
  12.0 13.2 %collective-permute-start.4 = (f32[138,4,128]{2,1,0:T(4,128)S(1)}, f32[138,4,128]{2,1,0:T(4,128)S(1)}, u32[]{:S(2)}, u32[]{:S(2)}) collective-permute-start(f32[138,4,128]{2,1,0:T(4,128)S(1)} %get-tuple-element.28), channel_id=1, source_target_pairs={{0,14},{2,0},{4,2},{6,4},{8,6},{10,8},{12,10},{14,12},{1,15},{3,1}... | collective-permute-start | bytes 847880 | tf_op jit(solution)/shard_map/ppermute | solution.py:388
  15.0 7.2 %collective-permute-start.1 = (f32[3,16,128]{2,1,0:T(8,128)S(1)}, f32[3,16,128]{2,1,0:T(8,128)S(1)}, u32[]{:S(2)}, u32[]{:S(2)}) collective-permute-start(f32[3,16,128]{2,1,0:T(8,128)S(1)} %get-tuple-element.21), channel_id=1, source_target_pairs={{16,1},{17,0},{32,17},{33,16},{48,33},{49,32},{64,49},{65,48},{80,... | collective-permute-start | bytes 73736 | tf_op jit(solution)/shard_map/ppermute | solution.py:374
  18.8 3.4 %copy-start.4 = (f32[2]{0:T(128)S(1)}, f32[2]{0:T(128)}, u32[]{:S(2)}) copy-start(f32[2]{0:T(128)} %param.9) | copy-start | bytes 28
  18.8 11.5 %collective-permute-start.7 = (f32[44,8,128]{2,1,0:T(8,128)S(1)}, f32[44,8,128]{2,1,0:T(8,128)S(1)}, u32[]{:S(2)}, u32[]{:S(2)}) collective-permute-start(f32[44,8,128]{2,1,0:T(8,128)S(1)} %get-tuple-element.35), channel_id=1, source_target_pairs={{16,0},{32,16},{48,32},{64,48},{80,64},{96,80},{112,96},{128,112},... | collective-permute-start | bytes 540680 | tf_op jit(solution)/shard_map/ppermute | solution.py:375
  22.3 6.4 %collective-permute-start.5 = (f32[47,4,128]{2,1,0:T(4,128)S(1)}, f32[47,4,128]{2,1,0:T(4,128)S(1)}, u32[]{:S(2)}, u32[]{:S(2)}) collective-permute-start(f32[47,4,128]{2,1,0:T(4,128)S(1)} %get-tuple-element.31), channel_id=1, source_target_pairs={{0,2},{2,4},{4,6},{6,8},{8,10},{10,12},{12,14},{14,0},{1,3},{3,5},... | collective-permute-start | bytes 288776 | tf_op jit(solution)/shard_map/ppermute | solution.py:394
  22.3 6.4 %collective-permute-start.6 = (f32[47,4,128]{2,1,0:T(4,128)S(1)}, f32[47,4,128]{2,1,0:T(4,128)S(1)}, u32[]{:S(2)}, u32[]{:S(2)}) collective-permute-start(f32[47,4,128]{2,1,0:T(4,128)S(1)} %get-tuple-element.32), channel_id=1, source_target_pairs={{0,14},{2,0},{4,2},{6,4},{8,6},{10,8},{12,10},{14,12},{1,15},{3,1}... | collective-permute-start | bytes 288776 | tf_op jit(solution)/shard_map/ppermute | solution.py:395
